TPU v7x, 32 devices: a whole 2x2x4 slice. The times are simulated.
32 devices in a mesh: dp: 2 (over x), seq: 16 (over z, y, core).
Axes of the slice: x: 2, y: 2, z: 4, core: 2. Of those that a mesh axis runs over, the one named last changes fastest.
Arguments:
- states: bfloat16 [4, 1024, 1152], P('dp', 'seq'), may hold values from -6 to 6
- counts: int32 [4, 4], P('dp'), may hold values from 0 to 1024, as said below
- cotangent: bfloat16 [4, 1024, 1152], P('dp', 'seq'), may hold values from -6 to 6
- w_qkv: bfloat16 [3, 1152, 1152], replicated, may hold values from -0.1875 to 0.1875
- w_out: bfloat16 [1152, 1152], replicated, may hold values from -1.5 to 1.5
- attn_bias: float32 [3, 1152], replicated, may hold values from -3 to 3
- norm_gain: float32 [2, 1152], replicated, may hold values from 0.25 to 1.75
- norm_bias: float32 [2, 1152], replicated, may hold values from -2 to 2
- w_up: bfloat16 [1152, 4304], replicated, may hold values from -0.1875 to 0.1875
- up_bias: float32 [4304], replicated, may hold values from -3 to 3
- w_down: bfloat16 [4304, 1152], replicated, may hold values from -0.09375 to 0.09375
- down_bias: float32 [1152], replicated, may hold values from -3 to 3
Outputs:
- layer_out: bfloat16 [4, 1024, 1152], P('dp', 'seq')
- state_grad: bfloat16 [4, 1024, 1152], P('dp', 'seq')
- grad_qkv: float32 [3, 1152, 1152], P(None, 'seq', 'dp')
- grad_out: float32 [1152, 1152], P('seq', 'dp')
- grad_attn_bias: float32 [3, 1152], P(None, 'seq')
- grad_gain: float32 [2, 1152], P(None, 'seq')
- grad_shift: float32 [2, 1152], P(None, 'seq')
- grad_up: float32 [1152, 4304], P('seq', 'dp')
- grad_up_bias: float32 [4304], P('seq')
- grad_down: float32 [4304, 1152], P('seq', 'dp')
- grad_down_bias: float32 [1152], P('seq')
Inputs may be any that keep to these rules, and one draw needn't show every extreme that they name: A group's 4 slots give patch counts packed from position 0 in slot order: used slots come first and hold 256 or more patches each, unused slots hold 0; their sum is at most 1024 and the rest of the group is padding. In some group a single image fills all 1024 positions.
All inputs are finite; a program needn't handle non-finite values.
Results may differ from a plain program's by a relative error of at most 0.02.
Values may be sent and summed in bfloat16 or wider, within the bound.
A program may use at most 256 MiB of HBM per device.

v0:
```python
import functools
import math

import jax
import jax.numpy as jnp
from jax import lax
from jax.sharding import PartitionSpec as P

HEADS = 16


EPS = 1e-06
NEG = -1e30


def normalize(values):
    mean = jnp.mean(values, axis=-1, keepdims=True)
    centred = values - mean
    scale = lax.rsqrt(jnp.mean(centred * centred, axis=-1, keepdims=True) + EPS)
    return (centred * scale, scale)


def norm_back(grad_norm, normed, scale, gain):
    scaled = grad_norm * gain
    return scale * (
        scaled
        - jnp.mean(scaled, axis=-1, keepdims=True)
        - normed * jnp.mean(scaled * normed, axis=-1, keepdims=True)
    )


def split_heads(tensor):
    groups, rows, width = tensor.shape
    return jnp.transpose(tensor.reshape(groups, rows, HEADS, width // HEADS), (2, 0, 1, 3))


def join_heads(tensor):
    heads, groups, rows, size = tensor.shape
    return jnp.transpose(tensor, (1, 2, 0, 3)).reshape(groups, rows, heads * size)


def ids_from(ends, offset, rows):
    positions = offset + jnp.arange(rows, dtype=jnp.int32)
    return jnp.sum((positions[None, :, None] >= ends[:, None, :]).astype(jnp.int32), axis=2)


def fold_keys(carry, piece, offset, query_heads, query_ids, ends):
    keys, values = piece
    key_ids = ids_from(ends, offset, keys.shape[1])
    same = query_ids[:, :, None] == key_ids[:, None, :]

    def one_head(args):
        query_head, key_head, value_head, highest, totals, accum = args
        scores = jnp.einsum(
            "gtd,gnd->gtn", query_head, key_head, preferred_element_type=jnp.float32
        )
        scores = jnp.where(same, scores, NEG)
        new_high = jnp.maximum(highest, jnp.max(scores, axis=-1))
        shrink = jnp.exp(highest - new_high)
        weights = jnp.where(same, jnp.exp(scores - new_high[..., None]), 0.0)
        totals = totals * shrink + jnp.sum(weights, axis=-1)
        accum = accum * shrink[..., None] + jnp.einsum(
            "gtn,gnd->gtd",
            weights.astype(jnp.bfloat16),
            value_head,
            preferred_element_type=jnp.float32,
        )
        return (new_high, totals, accum)

    highest, totals, accum = carry
    return lax.map(
        one_head, (query_heads, split_heads(keys), split_heads(values), highest, totals, accum)
    )


def score_grads(query_head, key_head, value_head, grad_head, log_head, delta_head, same):
    scores = jnp.einsum("gtd,gnd->gtn", query_head, key_head, preferred_element_type=jnp.float32)
    probs = jnp.where(same, jnp.exp(jnp.where(same, scores, NEG) - log_head[..., None]), 0.0)
    grad_probs = jnp.einsum(
        "gtd,gnd->gtn", grad_head, value_head, preferred_element_type=jnp.float32
    )
    grad_scores = (probs * (grad_probs - delta_head[..., None])).astype(jnp.bfloat16)
    return (probs, grad_scores)


def body(
    states,
    counts,
    cotangent,
    w_qkv,
    w_out,
    attn_bias,
    norm_gain,
    norm_bias,
    w_up,
    up_bias,
    w_down,
    down_bias,
):
    groups, rows, width = states.shape
    shards = lax.axis_size("seq")
    head_size = width // HEADS
    factor = 1.0 / math.sqrt(head_size)
    ends = jnp.cumsum(counts, axis=1)
    query_ids = ids_from(ends, lax.axis_index("seq") * rows, rows)
    valid = (query_ids < counts.shape[1]).astype(jnp.float32)[..., None]
    inputs = states.astype(jnp.float32)
    normed_one, scale_one = normalize(inputs)
    hidden_one = (normed_one * norm_gain[0] + norm_bias[0]).astype(jnp.bfloat16)
    projected = jnp.einsum("gtd,cde->cgte", hidden_one, w_qkv, preferred_element_type=jnp.float32)
    query = ((projected[0] + attn_bias[0]) * factor).astype(jnp.bfloat16)
    keys = projected[1].astype(jnp.bfloat16)
    values = (projected[2] + attn_bias[1]).astype(jnp.bfloat16)
    query_heads = split_heads(query)
    start_carry = (
        jnp.full((HEADS, groups, rows), NEG, jnp.float32),
        jnp.zeros((HEADS, groups, rows), jnp.float32),
        jnp.zeros((HEADS, groups, rows, head_size), jnp.float32),
    )
    folder = functools.partial(fold_keys, query_heads=query_heads, query_ids=query_ids, ends=ends)
    highest, totals, accum = folder(
        start_carry,
        (
            lax.all_gather(keys, "seq", axis=1, tiled=True),
            lax.all_gather(values, "seq", axis=1, tiled=True),
        ),
        jnp.int32(0),
    )
    attended = join_heads(accum / totals[..., None])
    log_total = highest + jnp.log(totals)
    attended_b = attended.astype(jnp.bfloat16)
    middle = (
        inputs
        + jnp.einsum("gtd,de->gte", attended_b, w_out, preferred_element_type=jnp.float32)
        + attn_bias[2]
    )
    normed_two, scale_two = normalize(middle)
    hidden_two = (normed_two * norm_gain[1] + norm_bias[1]).astype(jnp.bfloat16)
    hidden = (
        jnp.einsum("gtd,df->gtf", hidden_two, w_up, preferred_element_type=jnp.float32) + up_bias
    )
    activated, gelu_back = jax.vjp(functools.partial(jax.nn.gelu, approximate=True), hidden)
    activated_b = activated.astype(jnp.bfloat16)
    result = (
        middle
        + jnp.einsum("gtf,fd->gtd", activated_b, w_down, preferred_element_type=jnp.float32)
        + down_bias
    )
    layer_out = (result * valid).astype(jnp.bfloat16)
    grad_result = cotangent.astype(jnp.float32) * valid
    grad_result_b = grad_result.astype(jnp.bfloat16)
    grad_down_bias = jnp.sum(grad_result, axis=(0, 1))
    grad_down = jnp.einsum(
        "gtf,gtd->fd", activated_b, grad_result_b, preferred_element_type=jnp.float32
    )
    grad_activated = jnp.einsum(
        "gtd,fd->gtf", grad_result_b, w_down, preferred_element_type=jnp.float32
    )
    grad_hidden = gelu_back(grad_activated)[0].astype(jnp.bfloat16)
    grad_up_bias = jnp.sum(grad_hidden.astype(jnp.float32), axis=(0, 1))
    grad_up = jnp.einsum("gtd,gtf->df", hidden_two, grad_hidden, preferred_element_type=jnp.float32)
    grad_norm_two = jnp.einsum("gtf,df->gtd", grad_hidden, w_up, preferred_element_type=jnp.float32)
    gain_two = jnp.sum(grad_norm_two * normed_two, axis=(0, 1))
    shift_two = jnp.sum(grad_norm_two, axis=(0, 1))
    grad_middle = grad_result + norm_back(grad_norm_two, normed_two, scale_two, norm_gain[1])
    out_bias_grad = jnp.sum(grad_middle, axis=(0, 1))
    grad_middle_b = grad_middle.astype(jnp.bfloat16)
    grad_out = jnp.einsum(
        "gtd,gte->de", attended_b, grad_middle_b, preferred_element_type=jnp.float32
    )
    grad_att = jnp.einsum(
        "gte,de->gtd", grad_middle_b, w_out, preferred_element_type=jnp.float32
    ).astype(jnp.bfloat16)
    delta = jnp.sum(split_heads(grad_att.astype(jnp.float32) * attended), axis=-1)
    all_keys, all_values = (
        lax.all_gather(keys, "seq", axis=1, tiled=True),
        lax.all_gather(values, "seq", axis=1, tiled=True),
    )
    all_ids = ids_from(ends, 0, rows * shards)
    same = query_ids[:, :, None] == all_ids[:, None, :]

    def head_back(args):
        query_head, key_head, value_head, grad_head, log_head, delta_head = args
        probs, grad_scores = score_grads(
            query_head, key_head, value_head, grad_head, log_head, delta_head, same
        )
        grad_q = jnp.einsum(
            "gtn,gnd->gtd", grad_scores, key_head, preferred_element_type=jnp.float32
        )
        grad_k = jnp.einsum(
            "gtn,gtd->gnd", grad_scores, query_head, preferred_element_type=jnp.float32
        )
        grad_v = jnp.einsum(
            "gtn,gtd->gnd",
            probs.astype(jnp.bfloat16),
            grad_head,
            preferred_element_type=jnp.float32,
        )
        return (grad_q, grad_k, grad_v)

    grad_q_heads, grad_k_heads, grad_v_heads = lax.map(
        head_back,
        (
            query_heads,
            split_heads(all_keys),
            split_heads(all_values),
            split_heads(grad_att),
            log_total,
            delta,
        ),
    )
    grad_keys, grad_values = (
        lax.psum_scatter(
            join_heads(grad_k_heads).astype(jnp.bfloat16), "seq", scatter_dimension=1, tiled=True
        ).astype(jnp.float32),
        lax.psum_scatter(
            join_heads(grad_v_heads).astype(jnp.bfloat16), "seq", scatter_dimension=1, tiled=True
        ).astype(jnp.float32),
    )
    pre_grads = jnp.stack(
        [
            (join_heads(grad_q_heads) * factor).astype(jnp.bfloat16),
            grad_keys.astype(jnp.bfloat16),
            grad_values.astype(jnp.bfloat16),
        ]
    )
    grad_qkv = jnp.einsum(
        "gtd,cgte->cde", hidden_one, pre_grads, preferred_element_type=jnp.float32
    )
    bias_sums = jnp.sum(pre_grads.astype(jnp.float32), axis=(1, 2))
    grad_attn_bias = jnp.stack([bias_sums[0], bias_sums[2], out_bias_grad])
    grad_norm_one = jnp.einsum(
        "cgte,cde->gtd", pre_grads, w_qkv, preferred_element_type=jnp.float32
    )
    grad_gain = jnp.stack([jnp.sum(grad_norm_one * normed_one, axis=(0, 1)), gain_two])
    grad_shift = jnp.stack([jnp.sum(grad_norm_one, axis=(0, 1)), shift_two])
    state_grad = (
        grad_middle + norm_back(grad_norm_one, normed_one, scale_one, norm_gain[0])
    ).astype(jnp.bfloat16)
    (
        part_qkv,
        part_out,
        part_bias,
        part_gain,
        part_shift,
        part_up_bias,
        part_down_bias,
        part_up,
        part_down,
    ) = (
        lax.psum_scatter(
            grad_qkv.astype(jnp.bfloat16), "seq", scatter_dimension=1, tiled=True
        ).astype(jnp.float32),
        lax.psum_scatter(
            grad_out.astype(jnp.bfloat16), "seq", scatter_dimension=0, tiled=True
        ).astype(jnp.float32),
        lax.psum_scatter(
            grad_attn_bias.astype(jnp.bfloat16), "seq", scatter_dimension=1, tiled=True
        ).astype(jnp.float32),
        lax.psum_scatter(
            grad_gain.astype(jnp.bfloat16), "seq", scatter_dimension=1, tiled=True
        ).astype(jnp.float32),
        lax.psum_scatter(
            grad_shift.astype(jnp.bfloat16), "seq", scatter_dimension=1, tiled=True
        ).astype(jnp.float32),
        lax.psum_scatter(
            grad_up_bias.astype(jnp.bfloat16), "seq", scatter_dimension=0, tiled=True
        ).astype(jnp.float32),
        lax.psum_scatter(
            grad_down_bias.astype(jnp.bfloat16), "seq", scatter_dimension=0, tiled=True
        ).astype(jnp.float32),
        lax.psum_scatter(
            grad_up.astype(jnp.bfloat16), "seq", scatter_dimension=0, tiled=True
        ).astype(jnp.float32),
        lax.psum_scatter(
            grad_down.astype(jnp.bfloat16), "seq", scatter_dimension=0, tiled=True
        ).astype(jnp.float32),
    )
    matrices = (
        lax.psum_scatter(
            part_qkv.astype(jnp.bfloat16), "dp", scatter_dimension=2, tiled=True
        ).astype(jnp.float32),
        lax.psum_scatter(
            part_out.astype(jnp.bfloat16), "dp", scatter_dimension=1, tiled=True
        ).astype(jnp.float32),
        lax.psum_scatter(
            part_up.astype(jnp.bfloat16), "dp", scatter_dimension=1, tiled=True
        ).astype(jnp.float32),
        lax.psum_scatter(
            part_down.astype(jnp.bfloat16), "dp", scatter_dimension=1, tiled=True
        ).astype(jnp.float32),
    )
    vectors = lax.psum((part_bias, part_gain, part_shift, part_up_bias, part_down_bias), "dp")
    return (
        layer_out,
        state_grad,
        matrices[0],
        matrices[1],
        vectors[0],
        vectors[1],
        vectors[2],
        matrices[2],
        vectors[3],
        matrices[3],
        vectors[4],
    )


def solution(mesh):
    placed = (
        P("dp", "seq", None),
        P("dp", None),
        P("dp", "seq", None),
        P(),
        P(),
        P(),
        P(),
        P(),
        P(),
        P(),
        P(),
        P(),
    )
    return jax.shard_map(
        body,
        mesh=mesh,
        in_specs=placed,
        out_specs=(
            P("dp", "seq", None),
            P("dp", "seq", None),
            P(None, "seq", "dp"),
            P("seq", "dp"),
            P(None, "seq"),
            P(None, "seq"),
            P(None, "seq"),
            P("seq", "dp"),
            P("seq"),
            P("seq", "dp"),
            P("seq"),
        ),
        check_vma=False,
    )
```

profile of v0, /device:TPU:0, one launch (start us, length us, event | category | flops | bytes accessed | tf_op | source)
XLA Modules:
  0.0 963.1 jit_solution(5823856397816626613)
XLA Ops:
  12.6 4.8 fusion.75
  26.1 49.7 %all-gather.4.cloned.1.call-done = bf16[2,1024,1152]{2,1,0:T(8,128)(2,1)} async-done(((bf16[2,64,1152]{2,1,0:T(8,128)(2,1)}), bf16[2,1024,1152]{2,1,0:T(8,128)(2,1)}) %all-gather.4.cloned.1.call-update) | async-done | bytes 4718608 | tf_op jit(solution)/shard_map/all_gather | solution.py:125
  75.8 6.6 copy.85
  82.4 5.3 copy.87
  87.7 42.9 %all-gather.6.cloned.1.call-done = bf16[1,2,1024,1152]{3,2,0,1:T(8,128)(2,1)} async-done(((bf16[1,2,64,1152]{3,2,0,1:T(8,128)(2,1)}), bf16[1,2,1024,1152]{3,2,0,1:T(8,128)(2,1)}) %all-gather.6.cloned.1.call-update) | async-done | bytes 4718608 | tf_op jit(solution)/shard_map/all_gather | solution.py:124
  130.6 6.6 copy.84
  137.2 5.3 copy.86
  143.6 64.2 %while.30 = (s32[]{:T(128)}, f32[16,2,64]{2,1,0:T(2,128)S(1)}, f32[16,2,64]{2,1,0:T(2,128)}, f32[16,2,64,72]{3,2,1,0:T(8,128)}, bf16[16,2,64,72]{3,2,1,0:T(8,128...) while((s32[]{:T(128)}, f32[16,2,64]{2,1,0:T(2,128)S(1)}, ...), condition=%wide.region_8.9_spmd.clone, body=%wide.region_5.8_spmd.clone.sunk | while | flops 39200384 | bytes 2298469 | solution.py:71
  144.9 1.9 fusion.186
  148.9 1.9 fusion.186
  152.9 1.9 fusion.186
  156.9 1.9 fusion.186
  160.9 1.9 fusion.186
  164.9 1.9 fusion.186
  168.9 1.9 fusion.186
  180.9 1.9 fusion.186
  188.9 1.9 fusion.186
  196.9 1.9 fusion.186
  200.9 1.9 fusion.186
  211.7 2.5 reshape.170
  216.2 6.8 fusion.72
  223.1 8.4 fusion.156
  231.5 2.4 multiply_reduce_fusion
  236.6 2.5 fusion.71
  241.8 103.1 %while.31 = (s32[]{:T(128)}, f32[16,2,64,72]{3,2,1,0:T(8,128)S(1)}, bf16[16,2,1024,72]{2,3,0,1:T(8,128)(2,1)}, bf16[16,2,1024,72]{2,3,0,1:T(8,128)(2,1)}, bf16[1...) while((s32[]{:T(128)}, f32[16,2,64,72]{3,2,1,0:T(8,128)S(1)}, ...), condition=%wide.region_15.16_spmd.clone, body=%wide.region_14.15_spmd.clone.sunk | while | flops 95420416 | bytes 4637825 | solution.py:201
  344.9 6.7 copy.95
  351.6 6.7 copy.97
  359.4 9.0 fusion.56
  368.3 120.2 %fusion.4 = bf16[272,1152]{1,0:T(8,128)(2,1)S(1)} fusion(bf16[4304,1152]{1,0:T(8,128)(2,1)} %fusion.56), kind=kCustom, calls=%all-reduce-scatter | all-reduce-scatter fusion | flops 5013505 | bytes 10543616
  488.6 10.6 %collective-permute-start = (bf16[45,1152]{1,0:T(8,128)(2,1)S(1)}, bf16[45,1152]{1,0:T(8,128)(2,1)S(1)}, u32[]{:S(2)}, u32[]{:S(2)}) collective-permute-start(bf16[45,1152]{1,0:T(8,128)(2,1)S(1)} %slice.58), channel_id=1, source_target_pairs={{0,1},{1,2},{2,3},{3,4},{4,5},{5,6},{6,7},{7,8},{8,9},{9,10},{10,1... | collective-permute-start | bytes 311048
  500.4 2.5 concatenate
  507.4 33.6 %reduce-scatter.24.cloned.1.call-done = bf16[2,64,1152]{2,1,0:T(8,128)(2,1)} async-done(((bf16[2,1024,1152]{2,1,0:T(8,128)(2,1)}), bf16[2,64,1152]{2,1,0:T(8,128)(2,1)}) %reduce-scatter.24.cloned.1.call-update) | async-done | bytes 294928 | tf_op jit(solution)/shard_map/reduce_scatter | solution.py:216
  541.0 6.6 fusion.58
  547.6 19.3 %copy.98 = bf16[3,1152,1152]{2,0,1:T(4,128)(2,1)} copy(bf16[3,1152,1152]{1,2,0:T(8,128)(2,1)} %fusion.58) | data formatting | bytes 15925248 | tf_op jit(solution)/shard_map/convert_element_type | solution.py:252
  568.2 5.5 fusion.55
  576.9 6.4 fusion.103
  587.3 6.1 fusion.130
  593.8 188.7 %all-reduce.15.cloned.1.call-done = bf16[3,1152,1152]{2,0,1:T(4,128)(2,1)} async-done(((bf16[3,1152,1152]{2,0,1:T(4,128)(2,1)}), bf16[3,1152,1152]{2,0,1:T(4,128)(2,1)}) %all-reduce.15.cloned.1.call-update) | async-done | bytes 7962640
  783.8 17.3 %copy.102 = bf16[3,72,1152]{0,1,2:T(8,128)(2,1)} copy(bf16[3,72,1152]{2,0,1:T(4,128)(2,1)S(1)} %constant_dynamic-slice_fusion.6) | data formatting | bytes 995328
  801.2 23.1 %reshape.185 = bf16[1152,216]{1,0:T(8,128)(2,1)} reshape(bf16[1152,72,3]{2,1,0:T(8,128)(2,1)} %bitcast.253) | data formatting | bytes 995328
  824.4 63.5 %all-reduce.11 = (bf16[3,1152]{1,0:T(4,128)(2,1)S(1)}, bf16[2,1152]{1,0:T(2,128)(2,1)S(1)}, bf16[2,1152]{1,0:T(2,128)(2,1)S(1)}, bf16[4304]{0:T(1024)(128)(2,1)S(1)}, bf16[1152]{0:T(1024)(128)(2,1)S(1)}) all-reduce(bf16[3,1152]{1,0:T(4,128)(2,1)S(1)} %pad_maximum_fusion.1, ...), channel_id=9, replica_groups=mesh['dp'=2,'seq'=16] {'seq'}, use_global_device_ids=true, to_apply=%region_26.27.clone | all-reduce | flops 13520 | bytes 54080
  888.2 15.5 %reduce-scatter.26.cloned.1.call-done = bf16[72,4304]{1,0:T(8,128)(2,1)} async-done(((bf16[1152,4304]{1,0:T(8,128)(2,1)}), bf16[72,4304]{1,0:T(8,128)(2,1)}) %reduce-scatter.26.cloned.1.call-update) | async-done | bytes 619792 | tf_op jit(solution)/shard_map/reduce_scatter | solution.py:272
  903.8 5.5 all-reduce.10
  910.4 10.4 %reduce-scatter.28.cloned.1.call-done = bf16[576,216]{1,0:T(8,128)(2,1)} async-done(((bf16[1152,216]{1,0:T(8,128)(2,1)}), bf16[576,216]{1,0:T(8,128)(2,1)}) %reduce-scatter.28.cloned.1.call-update) | async-done | bytes 248848
  920.8 10.3 %reshape.186 = bf16[576,72,3]{2,1,0:T(8,128)(2,1)} reshape(bf16[576,216]{1,0:T(8,128)(2,1)} %reduce-scatter.28.cloned.1.call-done) | data formatting | bytes 497664
  931.1 11.3 %copy.103 = bf16[3,72,576]{2,0,1:T(4,128)(2,1)S(1)} copy(bf16[3,72,576]{0,1,2:T(8,128)(2,1)} %bitcast.256) | data formatting | bytes 497664
  943.3 10.8 %all-reduce.17.cloned.1.call-done = bf16[72,4304]{1,0:T(8,128)(2,1)} async-done(((bf16[72,4304]{1,0:T(8,128)(2,1)}), bf16[72,4304]{1,0:T(8,128)(2,1)}) %all-reduce.17.cloned.1.call-update) | async-done | bytes 619792
  954.1 2.0 dynamic-slice_convert_fusion
  (374 shorter events, 187.8 us)
Async XLA Ops:
  7.2 207.0 %copy-start = (bf16[1152,1152]{1,0:T(8,128)(2,1)S(1)}, bf16[1152,1152]{1,0:T(8,128)(2,1)}, u32[]{:S(2)}) copy-start(bf16[1152,1152]{1,0:T(8,128)(2,1)} %param.20) | copy-start | bytes 7962628
  7.2 68.6 %all-gather.4.cloned.1.call-start = ((), (), s32[]{:S(2)}) async-start(), calls=%async_computation.7 | async-start | bytes 5013504 | tf_op jit(solution)/shard_map/all_gather | solution.py:125
  8.5 8.9 copy-start.34
  9.7 7.8 copy-start.42
  12.6 4.8 copy-start.22
  12.6 4.9 copy-start.29
  17.5 6.0 copy-start.48
  19.5 111.1 %all-gather.6.cloned.1.call-start = ((), (), s32[]{:S(2)}) async-start(), calls=%async_computation.11 | async-start | bytes 5013504 | tf_op jit(solution)/shard_map/all_gather | solution.py:124
  21.4 484.0 %reduce-scatter.34.cloned.1.call-start = ((), (), s32[]{:S(2)}) async-start(), calls=%async_computation.17 | async-start | bytes 2820096
  207.8 6.3 copy-start.12
  207.9 6.3 copy-start.20
  208.4 5.7 copy-start.6
  215.9 17.9 %copy-start.25 = (f32[2,64]{1,0:T(2,128)}, f32[2,64]{1,0:T(2,128)S(1)}, u32[]{:S(2)}) copy-start(f32[2,64]{1,0:T(2,128)S(1)} %broadcast_multiply_fusion.4) | copy-start | bytes 1540
  216.1 17.7 %copy-start.27 = (f32[2,64]{1,0:T(2,128)}, f32[2,64]{1,0:T(2,128)S(1)}, u32[]{:S(2)}) copy-start(f32[2,64]{1,0:T(2,128)S(1)} %add_rsqrt_fusion) | copy-start | bytes 1540
  216.2 6.8 copy-start.14
  216.2 6.8 copy-start.45
  216.2 15.2 %slice-start = ((s8[9916416]{0:T(1024)(128)(4,1)}), s8[4194304]{0:T(1024)(128)(4,1)S(1)}, s32[]{:S(2)}) async-start(s8[9916416]{0:T(1024)(128)(4,1)} %bitcast.254), calls=%async_computation.18 | async-start | bytes 8388608
  216.2 15.2 %slice-start.1 = ((s8[9916416]{0:T(1024)(128)(4,1)}), s8[4194304]{0:T(1024)(128)(4,1)S(1)}, s32[]{:S(2)}) async-start(s8[9916416]{0:T(1024)(128)(4,1)} %bitcast.254), calls=%async_computation.19 | async-start | bytes 8388608
  223.0 8.4 copy-start.10
  223.0 8.4 slice-start.2
  231.4 3.3 copy-start.3
  236.6 3.8 copy-start.13
  241.6 265.8 %reduce-scatter.22.cloned.1.call-start = ((), (), s32[]{:S(2)}) async-start(), calls=%async_computation.8 | async-start | bytes 5013504 | tf_op jit(solution)/shard_map/reduce_scatter | solution.py:213
  351.6 189.4 %reduce-scatter.24.cloned.1.call-start = ((), (), s32[]{:S(2)}) async-start(), calls=%async_computation.9 | async-start | bytes 5013504 | tf_op jit(solution)/shard_map/reduce_scatter | solution.py:216
  358.4 225.0 %reduce-scatter.32.cloned.1.call-start = ((), (), s32[]{:S(2)}) async-start(), calls=%async_computation.14 | async-start | bytes 1327104
  368.3 130.8 %copy-start.47 = (u32[32]{0:T(128)S(1)}, u32[32]{0:T(128)}, u32[]{:S(2)}) copy-start(u32[32]{0:T(128)} %constant.97) | copy-start | bytes 388
  488.6 11.9 %collective-permute-start = (bf16[45,1152]{1,0:T(8,128)(2,1)S(1)}, bf16[45,1152]{1,0:T(8,128)(2,1)S(1)}, u32[]{:S(2)}, u32[]{:S(2)}) collective-permute-start(bf16[45,1152]{1,0:T(8,128)(2,1)S(1)} %slice.58), channel_id=1, source_target_pairs={{0,1},{1,2},{2,3},{3,4},{4,5},{5,6},{6,7},{7,8},{8,9},{9,10},{10,1... | collective-permute-start | bytes 311048
  504.3 36.7 %copy-start.23 = (f32[1152]{0:T(1024)S(1)}, f32[1152]{0:T(1024)}, u32[]{:S(2)}) copy-start(f32[1152]{0:T(1024)} %copy-done.22) | copy-start | bytes 13828
  504.3 36.7 %copy-start.30 = (f32[1152]{0:T(1024)S(1)}, f32[1152]{0:T(1024)}, u32[]{:S(2)}) copy-start(f32[1152]{0:T(1024)} %copy-done.29) | copy-start | bytes 13828
  504.3 36.7 %copy-start.35 = (f32[2,64]{1,0:T(2,128)S(1)}, f32[2,64]{1,0:T(2,128)}, u32[]{:S(2)}) copy-start(f32[2,64]{1,0:T(2,128)} %copy-done.34) | copy-start | bytes 1540
  504.3 36.7 %copy-start.43 = (f32[2,64]{1,0:T(2,128)S(1)}, f32[2,64]{1,0:T(2,128)}, u32[]{:S(2)}) copy-start(f32[2,64]{1,0:T(2,128)} %copy-done.42) | copy-start | bytes 1540
  504.4 81.1 %reduce-scatter.30.cloned.1.call-start = ((), (), s32[]{:S(2)}) async-start(), calls=%async_computation.13 | async-start | bytes 442368
  507.3 275.2 %all-reduce.15.cloned.1.call-start = ((), (), s32[]{:S(2)}) async-start(), calls=%async_computation.15 | async-start | bytes 21233664
  566.9 336.8 %reduce-scatter.26.cloned.1.call-start = ((), (), s32[]{:S(2)}) async-start(), calls=%async_computation.10 | async-start | bytes 10653696 | tf_op jit(solution)/shard_map/reduce_scatter | solution.py:272
  573.7 3.2 copy-start.33
  573.7 3.2 copy-start.32
  573.7 3.2 copy-start.11
  573.7 3.2 copy-start.49
  573.7 347.1 %reduce-scatter.28.cloned.1.call-start = ((), (), s32[]{:S(2)}) async-start(), calls=%async_computation.12 | async-start | bytes 884736
  576.9 10.4 %copy-start.44 = (f32[2,64]{1,0:T(2,128)S(1)}, f32[2,64]{1,0:T(2,128)}, u32[]{:S(2)}) copy-start(f32[2,64]{1,0:T(2,128)} %copy-done.42) | copy-start | bytes 1540
  587.3 6.2 copy-start.16
  587.3 6.2 copy-start.17
  801.2 23.2 %copy-start.38 = (bf16[1152]{0:T(1024)(128)(2,1)S(1)}, bf16[1152]{0:T(1024)(128)(2,1)}, u32[]{:S(2)}) copy-start(bf16[1152]{0:T(1024)(128)(2,1)} %get-tuple-element.386) | copy-start | bytes 6916
  801.2 23.2 %copy-start.41 = (bf16[4304]{0:T(1024)(128)(2,1)S(1)}, bf16[4304]{0:T(1024)(128)(2,1)}, u32[]{:S(2)}) copy-start(bf16[4304]{0:T(1024)(128)(2,1)} %get-tuple-element.397) | copy-start | bytes 25828
  801.2 108.2 %copy-start.5 = (f32[2,64,1152]{2,1,0:T(8,128)S(1)}, f32[2,64,1152]{2,1,0:T(8,128)}, u32[]{:S(2)}) copy-start(f32[2,64,1152]{2,1,0:T(8,128)} %copy-done.4) | copy-start | bytes 1769476
  801.2 108.2 %copy-start.36 = (f32[2,64]{1,0:T(2,128)S(1)}, f32[2,64]{1,0:T(2,128)}, u32[]{:S(2)}) copy-start(f32[2,64]{1,0:T(2,128)} %copy-done.34) | copy-start | bytes 1540
  824.3 129.9 %all-reduce.17.cloned.1.call-start = ((), (), s32[]{:S(2)}) async-start(), calls=%async_computation.16 | async-start | bytes 1253376
  931.1 24.9 %copy-start.1 = (bf16[1152,1152]{1,0:T(8,128)(2,1)S(1)}, bf16[1152,1152]{1,0:T(8,128)(2,1)}, u32[]{:S(2)}) copy-start(bf16[1152,1152]{1,0:T(8,128)(2,1)} %param.20) | copy-start | bytes 7962628
  (19 other events, 30.1 us)
Sparse Core Ops, SparseCore 0:
  19.6 56.1 all-gather.3
  78.6 51.9 all-gather.5
  241.7 62.5 reduce-scatter.33
  351.7 105.4 reduce-scatter.21
  460.9 80.0 reduce-scatter.23
  543.2 17.5 reduce-scatter.31
  563.7 12.0 reduce-scatter.29
  580.0 202.5 all-reduce.14
  786.7 116.9 reduce-scatter.25
  906.4 14.3 reduce-scatter.27
  923.3 30.8 all-reduce.16
where the time goes:
time: 974 us; the launch traced here: 963 us
  waiting for transfers between devices  352 us (36%)
  matrix products  214 us (22%)
  blocking collectives  189 us (19%)
  local copies, waits for them, and re-layouts  149 us (15%)
  other arithmetic  27.9 us (3%)
  between operations  17.7 us (2%)
  starting transfers between devices  11.3 us (1%)
    unnamed x18, waiting for transfers between devices  210 us
    unnamed x2, blocking collectives  184 us
    unnamed x126, local copies, waits for them, and re-layouts  88.4 us
    all_gather x1, waiting for transfers between devices, body(): lax.all_gather(values, 'seq', axis=1, tiled=True)  49.7 us
    all_gather x1, waiting for transfers between devices, body(): lax.all_gather(keys, 'seq', axis=1, tiled=True)  42.9 us
    reduce_scatter x1, waiting for transfers between devices, body(): lax.psum_scatter(join_heads(grad_v_heads).astype(jnp.bfloat16), 'seq', sc...  33.6 us
    dot_general x16, matrix products, one_head(): jnp.einsum('gtn,gnd->gtd', weights.astype(jnp.bfloat16), value_head, pref...  30.3 us
    dot_general x16, matrix products, head_back(): jnp.einsum('gtn,gtd->gnd', grad_scores, query_head, preferred_element_typ...  28.2 us
  transfers between devices with their start and end apart: 12, of which 7 were waited for; matrix products, arithmetic and copies ran while one was open for 40% of the time, Pallas kernels for 0%

commit v1 on v0

v1 whole, which is shorter than its diff:
```python
import functools
import math

import jax
import jax.numpy as jnp
from jax import lax
from jax.sharding import PartitionSpec as P

HEADS = 16
EPS = 1e-06
NEG = -1e30
F32 = jnp.float32
BF16 = jnp.bfloat16


def mm(spec, a, b):
    return jnp.einsum(spec, a, b, preferred_element_type=F32)


def normalize(values):
    mean = jnp.mean(values, axis=-1, keepdims=True)
    centred = values - mean
    scale = lax.rsqrt(jnp.mean(centred * centred, axis=-1, keepdims=True) + EPS)
    return (centred * scale, scale)


def norm_back(grad_norm, normed, scale, gain):
    scaled = grad_norm * gain
    return scale * (
        scaled
        - jnp.mean(scaled, axis=-1, keepdims=True)
        - normed * jnp.mean(scaled * normed, axis=-1, keepdims=True)
    )


def body(
    states, counts, cotangent, w_qkv, w_out, attn_bias, norm_gain, norm_bias,
    w_up, up_bias, w_down, down_bias,
):
    groups, rows, width = states.shape
    shards = lax.axis_size("seq")
    me = lax.axis_index("seq")
    size = width // HEADS
    ff = w_up.shape[1] // shards
    total = rows * shards
    factor = 1.0 / math.sqrt(size)
    ends = jnp.cumsum(counts, axis=1)
    ids = jnp.sum(
        (jnp.arange(total, dtype=jnp.int32)[None, :, None] >= ends[:, None, :]).astype(jnp.int32), axis=2
    )
    valid_all = (ids < counts.shape[1]).astype(F32)[..., None]
    valid = lax.dynamic_slice_in_dim(valid_all, me * rows, rows, 1)
    same = ids[:, :, None] == ids[:, None, :]

    def gather(x):
        return lax.all_gather(x, "seq", axis=1, tiled=True)

    wq = lax.dynamic_slice_in_dim(w_qkv, me * size, size, 2)
    wo = lax.dynamic_slice_in_dim(w_out, me * size, size, 0)
    wu = lax.dynamic_slice_in_dim(w_up, me * ff, ff, 1)
    wd = lax.dynamic_slice_in_dim(w_down, me * ff, ff, 0)
    bq = lax.dynamic_slice_in_dim(attn_bias, me * size, size, 1)
    bu = lax.dynamic_slice_in_dim(up_bias, me * ff, ff, 0)

    inputs = states.astype(F32)
    normed_one, scale_one = normalize(inputs)
    h1 = gather((normed_one * norm_gain[0] + norm_bias[0]).astype(BF16))
    grad_y = cotangent.astype(F32) * valid
    gy = gather(grad_y.astype(BF16))

    proj = mm("gtd,cde->cgte", h1, wq)
    query = ((proj[0] + bq[0]) * factor).astype(BF16)
    key = proj[1].astype(BF16)
    value = (proj[2] + bq[1]).astype(BF16)
    scores = jnp.where(same, mm("gqd,gkd->gqk", query, key), NEG)
    highest = jnp.max(scores, axis=-1, keepdims=True)
    weights = jnp.exp(scores - highest)
    totals = jnp.sum(weights, axis=-1, keepdims=True)
    attended = mm("gqk,gkd->gqd", weights.astype(BF16), value) / totals
    lse = highest + jnp.log(totals)
    att_b = attended.astype(BF16)
    att_mine = lax.all_to_all(att_b, "seq", split_axis=1, concat_axis=2, tiled=True)

    middle = inputs + mm("gtd,de->gte", att_mine, w_out) + attn_bias[2]
    normed_two, scale_two = normalize(middle)
    h2 = gather((normed_two * norm_gain[1] + norm_bias[1]).astype(BF16))
    hidden = mm("gtd,df->gtf", h2, wu) + bu
    act, gelu_back = jax.vjp(functools.partial(jax.nn.gelu, approximate=True), hidden)
    act_b = act.astype(BF16)
    down = lax.psum_scatter(
        mm("gtf,fd->gtd", act_b, wd).astype(BF16), "seq", scatter_dimension=1, tiled=True
    ).astype(F32)
    layer_out = ((middle + down + down_bias) * valid).astype(BF16)

    grad_down = mm("gtf,gtd->fd", act_b, gy)
    grad_down_bias = jnp.sum(gy.astype(F32), axis=(0, 1))
    grad_hidden = gelu_back(mm("gtd,fd->gtf", gy, wd))[0].astype(BF16)
    grad_up_bias = jnp.sum(grad_hidden.astype(F32), axis=(0, 1))
    grad_up = mm("gtd,gtf->df", h2, grad_hidden)
    grad_h2 = lax.psum_scatter(
        mm("gtf,df->gtd", grad_hidden, wu).astype(BF16), "seq", scatter_dimension=1, tiled=True
    ).astype(F32)
    gain_two = jnp.sum(grad_h2 * normed_two, axis=(0, 1))
    shift_two = jnp.sum(grad_h2, axis=(0, 1))
    grad_mid = grad_y + norm_back(grad_h2, normed_two, scale_two, norm_gain[1])
    out_bias = jnp.sum(grad_mid, axis=(0, 1))
    gm = gather(grad_mid.astype(BF16))
    grad_out = mm("gtd,gte->de", att_b, gm)
    grad_att = mm("gte,de->gtd", gm, wo).astype(BF16)

    delta = jnp.sum(grad_att.astype(F32) * attended, axis=-1, keepdims=True)
    scores2 = jnp.where(same, mm("gqd,gkd->gqk", query, key), NEG)
    probs = jnp.exp(scores2 - lse)
    grad_scores = (probs * (mm("gqd,gkd->gqk", grad_att, value) - delta)).astype(BF16)
    pre = jnp.stack(
        [
            (mm("gqk,gkd->gqd", grad_scores, key) * factor).astype(BF16),
            mm("gqk,gqd->gkd", grad_scores, query).astype(BF16),
            mm("gqk,gqd->gkd", probs.astype(BF16), grad_att).astype(BF16),
        ]
    )
    bias_sums = jnp.sum(pre.astype(F32), axis=(1, 2))
    grad_qkv = mm("gtd,cgte->cde", h1, pre)
    pre_mine = lax.all_to_all(pre, "seq", split_axis=2, concat_axis=3, tiled=True)
    grad_h1 = mm("cgte,cde->gtd", pre_mine, w_qkv)
    gain_one = jnp.sum(grad_h1 * normed_one, axis=(0, 1))
    shift_one = jnp.sum(grad_h1, axis=(0, 1))
    state_grad = (grad_mid + norm_back(grad_h1, normed_one, scale_one, norm_gain[0])).astype(BF16)

    qkv_rows = lax.all_to_all(grad_qkv.astype(BF16), "seq", split_axis=1, concat_axis=2, tiled=True)
    up_rows = lax.all_to_all(grad_up.astype(BF16), "seq", split_axis=0, concat_axis=1, tiled=True)
    wide = jnp.concatenate(
        [qkv_rows.reshape(-1, width), grad_out.astype(BF16), grad_down.astype(BF16)], axis=0
    )
    wide = lax.psum_scatter(wide, "dp", scatter_dimension=1, tiled=True).astype(F32)
    up_part = lax.psum_scatter(up_rows, "dp", scatter_dimension=1, tiled=True).astype(F32)
    vectors = lax.psum(jnp.stack([gain_one, gain_two, shift_one, shift_two, out_bias]), ("dp", "seq"))
    vectors = lax.dynamic_slice_in_dim(vectors, me * size, size, 1)
    pairs = lax.psum(
        (
            jnp.stack(
                [bias_sums[0], bias_sums[2], lax.dynamic_slice_in_dim(grad_down_bias, me * size, size, 0)]
            ),
            grad_up_bias,
        ),
        "dp",
    )
    narrow = wide.shape[1]
    return (
        layer_out,
        state_grad,
        wide[: 3 * size].reshape(3, size, narrow),
        wide[3 * size : 4 * size],
        jnp.stack([pairs[0][0], pairs[0][1], vectors[4]]),
        vectors[0:2],
        vectors[2:4],
        up_part,
        pairs[1],
        wide[4 * size :],
        pairs[0][2],
    )


def solution(mesh):
    placed = (P("dp", "seq", None), P("dp", None), P("dp", "seq", None)) + (P(),) * 9
    return jax.shard_map(
        body,
        mesh=mesh,
        in_specs=placed,
        out_specs=(
            P("dp", "seq", None), P("dp", "seq", None), P(None, "seq", "dp"), P("seq", "dp"),
            P(None, "seq"), P(None, "seq"), P(None, "seq"), P("seq", "dp"), P("seq"),
            P("seq", "dp"), P("seq"),
        ),
        check_vma=False,
    )
```

time: 974 us -> 609 us (0.63)
  blocking collectives: 189 us -> 45.5 us
  matrix products: 214 us -> 72.6 us
  local copies, waits for them, and re-layouts: 149 us -> 48.4 us
  waiting for transfers between devices: 352 us -> 375 us
    unnamed x18 -> x10, waiting for transfers between devices: 210 us -> 15.4 us
    unnamed x2 -> x0, blocking collectives: 184 us -> none
    dot_general x124 -> x18, matrix products: 214 us -> 72.6 us  [mm(): return jnp.einsum(spec, a, b, preferred_element_type=F32)]
    all_gather x2 -> x4, waiting for transfers between devices: 92.6 us -> 201 us  [gather(): return lax.all_gather(x, 'seq', axis=1, tiled=True)]
    reduce_scatter x3 -> x2, waiting for transfers between devices: 49.1 us -> 143 us  [the longest x1 75.8 us: body(): lax.psum_scatter(mm('gtf,fd->gtd', act_b, wd).astype(BF16), 'seq', scatte...]
    unnamed x126 -> x85, local copies, waits for them, and re-layouts: 88.4 us -> 16.3 us
    psum x1 -> x2, blocking collectives: 5.55 us -> 45.5 us  [the longest x1 40 us: body(): lax.psum(jnp.stack([gain_one, gain_two, shift_one, shift_two, out_bias]),...]
    convert_element_type x5 -> x3, local copies, waits for them, and re-layouts: 33.6 us -> 4.34 us  [the longest x1 2.4 us: body(): grad_up.astype(BF16)]
  transfers between devices with their start and end apart: 12 -> 12, of which waited for: 7 -> 9; matrix products, arithmetic and copies ran while one was open for 40% -> 15% of each run, Pallas kernels for 0% -> 0%
where the time goes in v1:
time: 609 us; the launch traced here: 601 us
  waiting for transfers between devices  375 us (62%)
  matrix products  72.6 us (12%)
  local copies, waits for them, and re-layouts  48.4 us (8%)
  blocking collectives  45.5 us (7%)
  other arithmetic  27.1 us (4%)
  starting transfers between devices  16.4 us (3%)
  between operations  15.9 us (3%)
    all_gather x4, waiting for transfers between devices, gather(): return lax.all_gather(x, 'seq', axis=1, tiled=True)  201 us
    reduce_scatter x1, waiting for transfers between devices, body(): lax.psum_scatter(mm('gtf,fd->gtd', act_b, wd).astype(BF16), 'seq', scatte...  75.8 us
    dot_general x18, matrix products, mm(): return jnp.einsum(spec, a, b, preferred_element_type=F32)  72.6 us
    reduce_scatter x1, waiting for transfers between devices, body(): lax.psum_scatter(mm('gtf,df->gtd', grad_hidden, wu).astype(BF16), 'seq',...  66.8 us
    psum x1, blocking collectives, body(): lax.psum(jnp.stack([gain_one, gain_two, shift_one, shift_two, out_bias]),...  40 us
    unnamed x85, local copies, waits for them, and re-layouts  16.3 us
    unnamed x10, waiting for transfers between devices  15.4 us
    all_to_all x1, waiting for transfers between devices, body(): lax.all_to_all(att_b, 'seq', split_axis=1, concat_axis=2, tiled=True)  13 us
  transfers between devices with their start and end apart: 12, of which 9 were waited for; matrix products, arithmetic and copies ran while one was open for 15% of the time, Pallas kernels for 0%

profile of v1, /device:TPU:0, one launch (start us, length us, event | category | flops | bytes accessed | tf_op | source)
XLA Modules:
  0.0 601.0 jit_solution(10767304804251223636)
XLA Ops:
  11.1 1.9 fusion.76
  14.8 54.5 %all-gather.5.cloned.1.call-done = bf16[2,1024,1152]{2,1,0:T(8,128)(2,1)} async-done(((bf16[2,64,1152]{2,1,0:T(8,128)(2,1)}), bf16[2,1024,1152]{2,1,0:T(8,128)(2,1)}) %all-gather.5.cloned.1.call-update) | async-done | bytes 4718608 | tf_op jit(solution)/shard_map/all_gather | solution.py:56
  69.4 5.3 fusion.44
  76.2 1.8 fusion.2
  79.4 2.8 fusion.121
  83.3 3.6 all-to-all-start
  88.3 13.0 %all-to-all-done = bf16[2,1024,72]{2,0,1:T(2,128)(2,1)S(1)} async-done(((bf16[2,1024,72]{2,0,1:T(2,128)(2,1)}), bf16[2,1024,72]{2,0,1:T(2,128)(2,1)S(1)}, u32[]{:S(2)}, u32[]{:S(2)}) %all-to-all-start) | async-done | bytes 294944 | tf_op jit(solution)/shard_map/all_to_all | solution.py:82
  102.4 2.3 all_to_all.54
  104.7 1.7 fusion.122
  108.8 1.8 fusion.94
  112.2 48.8 %all-gather.7.cloned.1.call-done = bf16[2,1024,1152]{2,1,0:T(8,128)(2,1)} async-done(((bf16[2,64,1152]{2,1,0:T(8,128)(2,1)}), bf16[2,1024,1152]{2,1,0:T(8,128)(2,1)}) %all-gather.7.cloned.1.call-update) | async-done | bytes 4718608 | tf_op jit(solution)/shard_map/all_gather | solution.py:56
  161.0 5.5 fusion.73
  166.5 49.3 %all-gather.9.cloned.1.call-done = bf16[2,1024,1152]{2,1,0:T(8,128)(2,1)} async-done(((bf16[2,64,1152]{2,1,0:T(8,128)(2,1)}), bf16[2,1024,1152]{2,1,0:T(8,128)(2,1)}) %all-gather.9.cloned.1.call-update) | async-done | bytes 4718608 | tf_op jit(solution)/shard_map/all_gather | solution.py:56
  215.8 6.6 %convert_reduce_fusion.1 = (f32[269]{0:T(512)}, bf16[2,1024,269]{1,2,0:T(8,128)(2,1)S(1)}) fusion(f32[2,1024,269]{1,2,0:T(8,128)} %fusion.73, f32[269]{0:T(512)} %dynamic_slice.28, bf16[2,1024,1152]{2,1,0:T(8,128)(2,1)} %all-gather.9.cloned.1.call-done, bf16[4304,1152]{1,0:T(8,128)(2,1)} %param.22, s32[]{:T(128)S(6)} %select_n.22), kind=kOutput, calls=%fused_computation.42 | convolution fusion | flops 1281971968 | bytes 8678456 | tf_op jit(solution)/shard_map/gtd,fd->gtf/dot_general | solution.py:17
  223.5 5.6 convolution_convert_fusion
  229.1 7.4 %convolution_convert_fusion.1 = bf16[2,1024,1152]{2,1,0:T(8,128)(2,1)} fusion(bf16[4304,1152]{1,0:T(8,128)(2,1)} %param.22, s32[]{:T(128)S(6)} %select_n.22, f32[2,1024,269]{1,2,0:T(8,128)} %fusion.73, f32[269]{0:T(512)} %dynamic_slice.28), kind=kOutput, calls=%fused_computation.11 | convolution fusion | flops 1277169664 | bytes 7575556 | tf_op jit(solution)/shard_map/gtf,fd->gtd/dot_general | solution.py:17
  236.6 66.8 %reduce-scatter.9.cloned.1.call-done = bf16[2,64,1152]{2,1,0:T(8,128)(2,1)} async-done(((bf16[2,1024,1152]{2,1,0:T(8,128)(2,1)}), bf16[2,64,1152]{2,1,0:T(8,128)(2,1)}) %reduce-scatter.9.cloned.1.call-update) | async-done | bytes 294928 | tf_op jit(solution)/shard_map/reduce_scatter | solution.py:100
  303.4 1.9 fusion.88
  306.4 75.8 %reduce-scatter.7.cloned.1.call-done = bf16[2,64,1152]{2,1,0:T(8,128)(2,1)} async-done(((bf16[2,1024,1152]{2,1,0:T(8,128)(2,1)}), bf16[2,64,1152]{2,1,0:T(8,128)(2,1)}) %reduce-scatter.7.cloned.1.call-update) | async-done | bytes 294928 | tf_op jit(solution)/shard_map/reduce_scatter | solution.py:90
  382.2 2.9 fusion.117
  388.0 5.1 fusion.20
  393.1 2.4 copy.84
  395.5 4.5 all-to-all-start.3
  400.0 47.9 %all-gather.11.cloned.1.call-done = bf16[2,1024,1152]{2,1,0:T(8,128)(2,1)} async-done(((bf16[2,64,1152]{2,1,0:T(8,128)(2,1)}), bf16[2,1024,1152]{2,1,0:T(8,128)(2,1)}) %all-gather.11.cloned.1.call-update) | async-done | bytes 4718608 | tf_op jit(solution)/shard_map/all_gather | solution.py:56
  447.9 4.2 multiply_reduce_fusion
  452.2 5.3 multiply_convert_fusion
  459.8 2.2 fusion.53
  464.5 2.0 reshape.124
  466.5 3.6 all-to-all-start.2
  471.4 3.0 convert_reduce_fusion
  477.5 3.0 copy.79
  480.4 3.5 all-to-all-done.2
  484.0 4.0 all-to-all-start.1
  488.4 6.0 fusion.19
  494.4 15.3 %all-reduce.4.cloned.1.call-done = bf16[72,4304]{1,0:T(8,128)(2,1)} async-done(((bf16[72,4304]{1,0:T(8,128)(2,1)}), bf16[72,4304]{1,0:T(8,128)(2,1)}) %all-reduce.4.cloned.1.call-update) | async-done | bytes 619792
  509.6 2.0 dynamic-slice_convert_fusion
  511.6 3.9 fusion.36
  515.6 2.5 reshape.125
  518.0 1.7 copy.107
  520.8 2.2 pad_maximum_fusion
  523.0 2.6 copy.98
  525.7 5.5 all-reduce.1
  531.7 2.2 copy.106
  533.9 3.0 all_to_all.58
  536.9 6.0 fusion.82
  543.0 40.0 %psum.22 = f32[5,1152]{1,0:T(8,128)S(1)} all-reduce(f32[5,1152]{1,0:T(8,128)S(1)} %stack.51), channel_id=1, replica_groups=mesh['dp'=2,'seq'=16] {'dp','seq'}, use_global_device_ids=true, to_apply=%region_24.25 | all-reduce | flops 5760 | bytes 46080 | tf_op jit(solution)/shard_map/psum | solution.py:137
  587.4 2.1 slice.90
  591.4 2.3 copy.111
  (153 shorter events, 37.9 us)
Async XLA Ops:
  7.2 97.5 %copy-start = (bf16[1152,1152]{1,0:T(8,128)(2,1)S(1)}, bf16[1152,1152]{1,0:T(8,128)(2,1)}, u32[]{:S(2)}) copy-start(bf16[1152,1152]{1,0:T(8,128)(2,1)} %param.16) | copy-start | bytes 7962628
  7.2 62.2 %all-gather.5.cloned.1.call-start = ((), (), s32[]{:S(2)}) async-start(), calls=%async_computation.7 | async-start | bytes 5013504 | tf_op jit(solution)/shard_map/all_gather | solution.py:56
  8.5 66.2 %copy-start.19 = (f32[2,64]{1,0:T(2,128)}, f32[2,64]{1,0:T(2,128)S(1)}, u32[]{:S(2)}) copy-start(f32[2,64]{1,0:T(2,128)S(1)} %broadcast_multiply_fusion.5) | copy-start | bytes 1540
  9.7 65.0 %copy-start.22 = (f32[2,64]{1,0:T(2,128)}, f32[2,64]{1,0:T(2,128)S(1)}, u32[]{:S(2)}) copy-start(f32[2,64]{1,0:T(2,128)S(1)} %add_rsqrt_fusion.1) | copy-start | bytes 1540
  14.8 59.9 %copy-start.27 = (f32[72]{0:T(128)}, f32[72]{0:T(128)S(1)}, u32[]{:S(2)}) copy-start(f32[72]{0:T(128)S(1)} %get-tuple-element.35) | copy-start | bytes 868
  14.8 63.2 %copy-start.31 = (f32[72]{0:T(128)}, f32[72]{0:T(128)S(1)}, u32[]{:S(2)}) copy-start(f32[72]{0:T(128)S(1)} %get-tuple-element.34) | copy-start | bytes 868
  74.7 3.3 copy-start.4
  76.2 3.2 copy-start.2
  76.2 3.2 copy-start.13
  78.0 1.4 copy-start.18
  82.2 1.1 copy-start.8
  82.2 22.5 %copy-start.3 = (bf16[2,64,1152]{2,1,0:T(8,128)(2,1)S(1)}, bf16[2,64,1152]{2,1,0:T(8,128)(2,1)}, u32[]{:S(2)}) copy-start(bf16[2,64,1152]{2,1,0:T(8,128)(2,1)} %param.12) | copy-start | bytes 884740
  83.3 18.0 %all-to-all-start = ((bf16[2,1024,72]{2,0,1:T(2,128)(2,1)}), bf16[2,1024,72]{2,0,1:T(2,128)(2,1)S(1)}, u32[]{:S(2)}, u32[]{:S(2)}) async-start(bf16[2,1024,72]{2,0,1:T(2,128)(2,1)} %copy.72), calls=%async_computation | async-start | bytes 1048576 | tf_op jit(solution)/shard_map/all_to_all | solution.py:82
  86.9 74.1 %all-gather.7.cloned.1.call-start = ((), (), s32[]{:S(2)}) async-start(), calls=%async_computation.8 | async-start | bytes 5013504 | tf_op jit(solution)/shard_map/all_gather | solution.py:56
  104.7 2.5 copy-start.12
  104.7 2.5 copy-start.14
  108.1 107.7 %all-gather.9.cloned.1.call-start = ((), (), s32[]{:S(2)}) async-start(), calls=%async_computation.10 | async-start | bytes 5013504 | tf_op jit(solution)/shard_map/all_gather | solution.py:56
  110.6 192.8 %reduce-scatter.9.cloned.1.call-start = ((), (), s32[]{:S(2)}) async-start(), calls=%async_computation.11 | async-start | bytes 5013504 | tf_op jit(solution)/shard_map/reduce_scatter | solution.py:100
  222.4 1.0 copy-start.34
  229.1 153.1 %reduce-scatter.7.cloned.1.call-start = ((), (), s32[]{:S(2)}) async-start(), calls=%async_computation.9 | async-start | bytes 5013504 | tf_op jit(solution)/shard_map/reduce_scatter | solution.py:90
  236.5 211.4 %all-gather.11.cloned.1.call-start = ((), (), s32[]{:S(2)}) async-start(), calls=%async_computation.12 | async-start | bytes 5013504 | tf_op jit(solution)/shard_map/all_gather | solution.py:56
  385.1 0.8 copy-start.6
  393.1 54.8 %copy-start.11 = (f32[2,1024,72]{1,2,0:T(8,128)S(1)}, f32[2,1024,72]{1,2,0:T(8,128)}, u32[]{:S(2)}) copy-start(f32[2,1024,72]{1,2,0:T(8,128)} %get-tuple-element.39) | copy-start | bytes 1769476
  395.5 71.0 %all-to-all-start.3 = ((bf16[16,72,269]{2,1,0:T(8,128)(2,1)}), bf16[16,72,269]{2,1,0:T(8,128)(2,1)}, u32[]{:S(2)}, u32[]{:S(2)}) async-start(bf16[16,72,269]{2,1,0:T(8,128)(2,1)} %bitcast.180), calls=%async_computation.5 | async-start | bytes 1769472 | tf_op jit(solution)/shard_map/all_to_all | solution.py:131
  447.9 4.2 copy-start.26
  447.9 4.2 copy-start.32
  447.9 11.8 %slice-start = ((s8[8388608]{0:T(1024)(128)(4,1)}), s8[4194304]{0:T(1024)(128)(4,1)S(1)}, s32[]{:S(2)}) async-start(s8[8388608]{0:T(1024)(128)(4,1)} %bitcast.168), calls=%async_computation.15 | async-start | bytes 8388608
  452.1 5.3 copy-start.5
  452.1 5.3 copy-start.28
  452.2 7.6 %slice-start.1 = ((s8[8388608]{0:T(1024)(128)(4,1)}), s8[4194304]{0:T(1024)(128)(4,1)S(1)}, s32[]{:S(2)}) async-start(s8[8388608]{0:T(1024)(128)(4,1)} %bitcast.168), calls=%async_computation.16 | async-start | bytes 8388608
  458.9 3.3 slice-start.2
  459.8 2.4 slice-start.3
  463.6 6.6 %copy-start.33 = (u32[32]{0:T(128)S(1)}, u32[32]{0:T(128)}, u32[]{:S(2)}) copy-start(u32[32]{0:T(128)} %constant.57) | copy-start | bytes 388
  466.5 17.4 %all-to-all-start.2 = ((bf16[16,2,7776]{2,1,0:T(2,128)(2,1)}), bf16[16,2,7776]{2,1,0:T(2,128)(2,1)S(1)}, u32[]{:S(2)}, u32[]{:S(2)}) async-start(bf16[16,2,7776]{2,1,0:T(2,128)(2,1)} %reshape.124), calls=%async_computation.4 | async-start | bytes 999424 | tf_op jit(solution)/shard_map/all_to_all | solution.py:130
  470.1 39.5 %all-reduce.4.cloned.1.call-start = ((), (), s32[]{:S(2)}) async-start(), calls=%async_computation.14 | async-start | bytes 1253376
  477.5 10.9 %copy-start.30 = (f32[269]{0:T(512)S(1)}, f32[269]{0:T(512)}, u32[]{:S(2)}) copy-start(f32[269]{0:T(512)} %dynamic_slice.28) | copy-start | bytes 3232
  484.0 47.7 %all-to-all-start.1 = ((bf16[3,2,1024,72]{3,1,0,2:T(2,128)(2,1)}), bf16[3,2,1024,72]{3,1,0,2:T(2,128)(2,1)S(1)}, u32[]{:S(2)}, u32[]{:S(2)}) async-start(bf16[3,2,1024,72]{3,1,0,2:T(2,128)(2,1)} %copy.79), calls=%async_computation.3 | async-start | bytes 3145728 | tf_op jit(solution)/shard_map/all_to_all | solution.py:124
  488.0 23.6 %copy-start.16 = (f32[1152]{0:T(1024)S(1)}, f32[1152]{0:T(1024)}, u32[]{:S(2)}) copy-start(f32[1152]{0:T(1024)} %get-tuple-element.11) | copy-start | bytes 13828
  488.0 23.6 %copy-start.17 = (f32[1152]{0:T(1024)S(1)}, f32[1152]{0:T(1024)}, u32[]{:S(2)}) copy-start(f32[1152]{0:T(1024)} %get-tuple-element.27) | copy-start | bytes 13828
  488.0 23.6 %copy-start.15 = (f32[1152]{0:T(1024)S(1)}, f32[1152]{0:T(1024)}, u32[]{:S(2)}) copy-start(f32[1152]{0:T(1024)} %get-tuple-element.18) | copy-start | bytes 13828
  488.0 23.6 %copy-start.9 = (bf16[2,1024,72]{1,2,0:T(8,128)(2,1)S(1)}, bf16[2,1024,72]{1,2,0:T(8,128)(2,1)}, u32[]{:S(2)}) copy-start(bf16[2,1024,72]{1,2,0:T(8,128)(2,1)} %copy-done.8) | copy-start | bytes 884740
  488.0 97.2 %reduce-scatter.11.cloned.1.call-start = ((), (), s32[]{:S(2)}) async-start(), calls=%async_computation.13 | async-start | bytes 2211840
  518.0 2.7 copy-start.10
  523.0 2.6 copy-start.29
  531.7 5.2 copy-start.20
  531.7 5.2 copy-start.23
  536.9 47.3 %copy-start.7 = (f32[2,64,1152]{2,1,0:T(8,128)S(1)}, f32[2,64,1152]{2,1,0:T(8,128)}, u32[]{:S(2)}) copy-start(f32[2,64,1152]{2,1,0:T(8,128)} %copy-done.6) | copy-start | bytes 1769476
  586.3 7.5 %copy-start.1 = (bf16[1152,1152]{1,0:T(8,128)(2,1)S(1)}, bf16[1152,1152]{1,0:T(8,128)(2,1)}, u32[]{:S(2)}) copy-start(bf16[1152,1152]{1,0:T(8,128)(2,1)} %param.16) | copy-start | bytes 7962628
  (3 other events, 1.7 us)
Sparse Core Ops, SparseCore 0:
  13.2 56.1 all-gather.4
  108.2 52.7 all-gather.6
  163.8 51.9 all-gather.8
  229.2 74.1 reduce-scatter.8
  307.6 74.5 reduce-scatter.6
  386.8 61.0 all-gather.10
  477.5 32.0 all-reduce.3
  525.7 25.4 reduce-scatter.10

commit v2 on v1

v2 whole, which is shorter than its diff:
```python
import functools
import math

import jax
import jax.numpy as jnp
from jax import lax
from jax.experimental import pallas as pl
from jax.experimental.pallas import tpu as pltpu
from jax.sharding import PartitionSpec as P

HEADS = 16
EPS = 1e-06
NEG = -1e30
F32 = jnp.float32
BF16 = jnp.bfloat16
MESH = pl.DeviceIdType.MESH
VMEM = pltpu.VMEM
DMA = pltpu.SemaphoreType.DMA


def mm(spec, a, b):
    return jnp.einsum(spec, a, b, preferred_element_type=F32)


def dot(a, b, ca=1, cb=0):
    return lax.dot_general(a, b, (((ca,), (cb,)), ((), ())), preferred_element_type=F32)


def pad_to(x, axis, size):
    pads = [(0, 0)] * x.ndim
    pads[axis] = (0, size - x.shape[axis])
    return jnp.pad(x, pads)


def up128(n):
    return -(-n // 128) * 128


def normalize(values):
    mean = jnp.mean(values, axis=-1, keepdims=True)
    centred = values - mean
    scale = lax.rsqrt(jnp.mean(centred * centred, axis=-1, keepdims=True) + EPS)
    return (centred * scale, scale)


def norm_back(grad_norm, normed, scale, gain):
    scaled = grad_norm * gain
    return scale * (
        scaled
        - jnp.mean(scaled, axis=-1, keepdims=True)
        - normed * jnp.mean(scaled * normed, axis=-1, keepdims=True)
    )


def gelu_both(v):
    c, a = 0.7978845608028654, 0.044715
    sq = v * v
    t = jnp.tanh(c * (v + a * v * sq))
    half = 0.5 * (1.0 + t)
    return v * half, half + 0.5 * v * (1.0 - t * t) * (c * (1.0 + 3.0 * a * sq))


class Ring:
    def __init__(self, shards):
        self.n = shards // 2
        self.half = self.n // 2
        self.me = lax.axis_index("seq")
        self.chip = self.me // 2
        self.core = self.me % 2
        odd = self.chip % 2
        self.pos = (1 - odd) * (self.chip // 2) + odd * (self.n - 1 - self.chip // 2)
        self.to = (self.at(1, 1) * 2 + self.core, self.at(1, 0) * 2 + self.core)
        self.sib = self.chip * 2 + 1 - self.core

    def at(self, k, d):
        p = (self.pos + (self.n - k if d == 0 else k)) % self.n
        hi = p // self.half
        return (1 - hi) * 2 * p + hi * (2 * (self.n - 1 - p) + 1)

    def greet(self):
        bar = pltpu.get_barrier_semaphore()
        for d in self.to + (self.sib,):
            pl.semaphore_signal(bar, inc=1, device_id={"seq": d}, device_id_type=MESH)

    def met(self):
        pl.semaphore_wait(pltpu.get_barrier_semaphore(), 3)


def gather_sems(shards):
    return [DMA((2, shards // 4 + 1, 2))] * 4


class Gather:
    def __init__(self, ring, buf, sems):
        self.ring, self.buf = ring, buf
        self.ring_s, self.ring_r, self.sib_s, self.sib_r = sems
        self.sent = []

    def copy(self, k, d, g, to_sib):
        block = self.buf.at[self.ring.at(k, d) * 2 + self.ring.core, g]
        s, r = (self.sib_s, self.sib_r) if to_sib else (self.ring_s, self.ring_r)
        return pltpu.make_async_remote_copy(
            src_ref=block, dst_ref=block, send_sem=s.at[d, k, g], recv_sem=r.at[d, k, g],
            device_id={"seq": self.ring.sib if to_sib else self.ring.to[d]}, device_id_type=MESH,
        )

    def units(self, k):
        if k == self.ring.half:
            return [(0, 0), (1, 1)]
        return [(0, 0), (1, 1), (0, 1), (1, 0)]

    def hop(self, k):
        half = self.ring.half
        for d, g in self.units(k):
            if k > 0:
                self.copy(k - 1, d, g, False).wait_recv()
            if k < half - 1 or (k == half - 1 and g == d):
                c = self.copy(k, d, g, False)
                c.start()
                self.sent.append(c)
        for d, g in self.units(k):
            if k > 0 or d == g:
                c = self.copy(k, d, g, True)
                c.start()
                self.sent.append(c)

    def ready(self, k):
        for d, g in self.units(k):
            if k > 0 or d == g:
                self.copy(k, d, g, True).wait_recv()

    def blocks(self, k):
        if k == 0 or k == self.ring.half:
            return [self.ring.at(k, 0)]
        return [self.ring.at(k, 0), self.ring.at(k, 1)]

    def finish(self):
        for c in self.sent:
            c.wait_send()


def scatter_scratch(shards, rows, width):
    n = shards // 2
    return [
        VMEM((n, 2, rows, width), BF16), VMEM((2, n // 2, 2, rows, width), BF16),
        DMA((n,)), DMA((n,)), DMA((2, n // 2, 2)), DMA((2, n // 2, 2)),
    ]


class Scatter:
    def __init__(self, ring, part, scratch):
        self.ring, self.part = ring, part
        self.sib_land, self.land, self.sib_s, self.sib_r, self.ring_s, self.ring_r = scratch
        self.sent = []

    def slot(self, k, d):
        if k == 0:
            return 0
        return self.ring.n - 1 if k == self.ring.half else 2 * k - 1 + d

    def sib_copy(self, k, d):
        r, i = self.ring, self.slot(k, d)
        return pltpu.make_async_remote_copy(
            src_ref=self.part.at[r.at(k, d) * 2 + 1 - r.core], dst_ref=self.sib_land.at[i],
            send_sem=self.sib_s.at[i], recv_sem=self.sib_r.at[i],
            device_id={"seq": r.sib}, device_id_type=MESH,
        )

    def give(self, k, d):
        c = self.sib_copy(k, d)
        c.start()
        self.sent.append(c)

    def ring_copy(self, h, d, g):
        r = self.ring
        return pltpu.make_async_remote_copy(
            src_ref=self.part.at[r.at(r.half - h, 1 - d) * 2 + r.core, g], dst_ref=self.land.at[d, h, g],
            send_sem=self.ring_s.at[d, h, g], recv_sem=self.ring_r.at[d, h, g],
            device_id={"seq": r.to[d]}, device_id_type=MESH,
        )

    def hop(self, h):
        r = self.ring
        j = r.half - h
        order = [(0, 0), (1, 1)] if h == 0 else [(0, 0), (1, 1), (0, 1), (1, 0)]
        if h == 0:
            self.sib_copy(j, 0).wait_recv()
        else:
            self.sib_copy(j, 0).wait_recv()
            self.sib_copy(j, 1).wait_recv()
        for d, g in order:
            own = r.at(j, 1 - d) * 2 + r.core
            val = self.part[own, g].astype(F32) + self.sib_land[self.slot(j, 1 - d), g].astype(F32)
            if h >= 2 or (h == 1 and g == d):
                self.ring_copy(h - 1, d, g).wait_recv()
                val = val + self.land[d, h - 1, g].astype(F32)
            self.part[own, g] = val.astype(BF16)
            c = self.ring_copy(h, d, g)
            c.start()
            self.sent.append(c)

    def result(self):
        r = self.ring
        self.sib_copy(0, 0).wait_recv()
        out = []
        for g in range(2):
            val = self.part[r.me, g].astype(F32) + self.sib_land[0, g].astype(F32)
            for d in range(2):
                self.ring_copy(r.half - 1, d, g).wait_recv()
                val = val + self.land[d, r.half - 1, g].astype(F32)
            out.append(val)
        return jnp.concatenate(out, axis=0)

    def finish(self):
        for c in self.sent:
            c.wait_send()


def first_kernel(shards, x_ref, vec_ref, w_ref, b_ref, h_ref, qkv_ref, *sems):
    ring = Ring(shards)
    ring.greet()
    groups, rows, width = x_ref.shape
    normed, _ = normalize(x_ref[...].reshape(groups * rows, width).astype(F32))
    h = (normed * vec_ref[0:1] + vec_ref[1:2]).astype(BF16)
    h_ref[ring.me] = h.reshape(groups, rows, width)
    ring.met()
    gat = Gather(ring, h_ref, sems)

    def work(chip):
        block = h_ref[pl.ds(2 * chip, 2)].reshape(4 * rows, width)
        out = ((dot(block, w_ref[...]) + b_ref[0:1]) * b_ref[1:2]).astype(BF16)
        qkv_ref[pl.ds(2 * chip, 2)] = out.reshape(2, groups, rows, out.shape[1])

    gat.hop(0)
    for k in range(1, ring.half + 1):
        gat.ready(k - 1)
        for chip in gat.blocks(k - 1):
            work(chip)
        gat.hop(k)
    gat.ready(ring.half)
    for chip in gat.blocks(ring.half):
        work(chip)
    gat.finish()


def first(shards, states, vecs, weights, consts):
    groups, rows, width = states.shape
    wide = weights.shape[1]
    return pl.pallas_call(
        functools.partial(first_kernel, shards),
        out_shape=[
            jax.ShapeDtypeStruct((shards, groups, rows, width), BF16),
            jax.ShapeDtypeStruct((shards, groups, rows, wide), BF16),
        ],
        in_specs=[pl.BlockSpec(memory_space=VMEM)] * 4,
        out_specs=[pl.BlockSpec(memory_space=VMEM)] * 2,
        scratch_shapes=gather_sems(shards),
        name="first",
        compiler_params=pltpu.CompilerParams(
            collective_id=0, has_side_effects=True, vmem_limit_bytes=40 << 20
        ),
    )(states, vecs, weights, consts)


def middle_kernel(
    shards, att_ref, x_ref, gy_ref, atts_ref, vec_ref, bu_ref, wout_ref, wo_ref, wu_ref, wd_ref,
    mid_ref, gmid_ref, gatt_ref, gout_ref, gup_ref, gdown_ref, down_ref, sums_ref, bup_ref,
    h_buf, m_buf, part, act_buf, ghid_buf, gact_buf, *rest,
):
    ring = Ring(shards)
    ring.greet()
    groups, rows, width = x_ref.shape
    own = groups * rows
    gat = Gather(ring, h_buf, rest[0:4])
    gat2 = Gather(ring, m_buf, rest[4:8])
    sca = Scatter(ring, part, rest[8:14])
    half = ring.half
    mid = (
        x_ref[...].reshape(own, width).astype(F32)
        + dot(att_ref[...].reshape(own, width), wout_ref[...])
        + vec_ref[2:3]
    )
    mid_ref[...] = mid.reshape(groups, rows, width)
    normed, scale = normalize(mid)
    h_buf[ring.me] = (normed * vec_ref[0:1] + vec_ref[1:2]).astype(BF16).reshape(groups, rows, width)
    ring.met()

    def rows_of(ref, chip):
        return ref[pl.ds(2 * chip, 2)].reshape(4 * rows, ref.shape[-1])

    def put(ref, chip, val):
        ref[pl.ds(2 * chip, 2)] = val.astype(ref.dtype).reshape((2, groups, rows, ref.shape[-1]))

    def grad_act(chip):
        put(gact_buf, chip, dot(rows_of(gy_ref, chip), wd_ref[...], 1, 1))

    def forward(chip):
        hidden = dot(rows_of(h_buf, chip), wu_ref[...]) + bu_ref[...]
        act, slope = gelu_both(hidden)
        put(act_buf, chip, act)
        ghid = (rows_of(gact_buf, chip) * slope).astype(BF16)
        put(ghid_buf, chip, ghid)
        put(part, chip, dot(ghid, wu_ref[...], 1, 1))

    gat.hop(0)
    grad_act(ring.at(0, 0))
    for k in range(half):
        gat.ready(k)
        for d, chip in enumerate(gat.blocks(k)):
            forward(chip)
            sca.give(k, d)
        for chip in gat.blocks(k + 1):
            grad_act(chip)
        gat.hop(k + 1)
    gat.ready(half)
    forward(ring.at(half, 0))
    sca.give(half, 0)
    for h in range(half):
        sca.hop(h)
    grad_h2 = sca.result()
    mean_h = mid_ref[...].reshape(own, width)
    normed, scale = normalize(mean_h)
    gy_own = gy_ref[ring.me].reshape(own, width).astype(F32)
    gmid = gy_own + norm_back(grad_h2, normed, scale, vec_ref[0:1])
    gmid_ref[...] = gmid.reshape(groups, rows, width)
    m_buf[ring.me] = gmid.astype(BF16).reshape(groups, rows, width)
    gat2.hop(0)
    sums_ref[0:1] = jnp.sum(grad_h2 * normed, axis=0, keepdims=True)
    sums_ref[1:2] = jnp.sum(grad_h2, axis=0, keepdims=True)
    sums_ref[2:3] = jnp.sum(gmid, axis=0, keepdims=True)

    def back(chip, first_one):
        block = rows_of(m_buf, chip)
        put(gatt_ref, chip, dot(block, wo_ref[...], 1, 1))
        part_out = dot(rows_of(atts_ref, chip), block, 0, 0)
        gout_ref[...] = part_out if first_one else gout_ref[...] + part_out

    tokens = shards * own
    flat = lambda ref: ref[...].reshape(tokens, ref.shape[-1])

    def down_part(chip):
        put(down_ref, chip, dot(rows_of(act_buf, chip), wd_ref[...]))

    for k in range(half):
        if k == 0:
            sums_ref[3:4] = jnp.sum(flat(gy_ref).astype(F32), axis=0, keepdims=True)
            bup_ref[...] = jnp.sum(flat(ghid_buf).astype(F32), axis=0, keepdims=True)
            gdown_ref[...] = dot(flat(act_buf), flat(gy_ref), 0, 0)
        if k == 1:
            gup_ref[...] = dot(flat(ghid_buf), flat(h_buf), 0, 0)
        for chip in gat.blocks(k):
            down_part(chip)
        gat2.hop(k + 1)
        gat2.ready(k)
        for chip in gat2.blocks(k):
            back(chip, k == 0)
    down_part(ring.at(half, 0))
    gat2.ready(half)
    back(ring.at(half, 0), False)
    gat.finish()
    gat2.finish()
    sca.finish()


def middle(shards, att, states, gy, att_head, vecs, bu, w_out, wo, wu, wd):
    groups, rows, width = states.shape
    ffp, hp = wu.shape[1], wo.shape[0]
    blocks = (shards, groups, rows)
    sds = jax.ShapeDtypeStruct
    return pl.pallas_call(
        functools.partial(middle_kernel, shards),
        out_shape=[
            sds((groups, rows, width), F32), sds((groups, rows, width), F32), sds(blocks + (hp,), BF16),
            sds((hp, width), F32), sds((ffp, width), F32), sds((ffp, width), F32), sds(blocks + (width,), BF16),
            sds((8, width), F32), sds((1, ffp), F32),
        ],
        in_specs=[pl.BlockSpec(memory_space=VMEM)] * 10,
        out_specs=[pl.BlockSpec(memory_space=VMEM)] * 9,
        scratch_shapes=[
            VMEM(blocks + (width,), BF16), VMEM(blocks + (width,), BF16), VMEM(blocks + (width,), BF16),
            VMEM(blocks + (ffp,), BF16), VMEM(blocks + (ffp,), BF16), VMEM(blocks + (ffp,), F32),
        ]
        + gather_sems(shards) * 2
        + scatter_scratch(shards, rows, width),
        name="middle",
        compiler_params=pltpu.CompilerParams(
            collective_id=1, has_side_effects=True, vmem_limit_bytes=60 << 20
        ),
    )(att, states, gy, att_head, vecs, bu, w_out, wo, wu, wd)


def body(
    states, counts, cotangent, w_qkv, w_out, attn_bias, norm_gain, norm_bias,
    w_up, up_bias, w_down, down_bias,
):
    groups, rows, width = states.shape
    shards = lax.axis_size("seq")
    me = lax.axis_index("seq")
    size = width // HEADS
    sp = up128(size)
    ff = w_up.shape[1] // shards
    ffp = up128(ff)
    total = rows * shards
    factor = 1.0 / math.sqrt(size)
    ends = jnp.cumsum(counts, axis=1)
    ids = jnp.sum(
        (jnp.arange(total, dtype=jnp.int32)[None, :, None] >= ends[:, None, :]).astype(jnp.int32), axis=2
    )
    valid_all = (ids < counts.shape[1]).astype(F32)[..., None]
    valid = lax.dynamic_slice_in_dim(valid_all, me * rows, rows, 1)
    same = ids[:, :, None] == ids[:, None, :]

    def by_block(x):
        return jnp.transpose(x.reshape(groups, shards, rows, -1), (1, 0, 2, 3))

    def by_group(x):
        return jnp.transpose(x, (1, 0, 2, 3)).reshape(groups, total, -1)

    def mine(x, axis, count):
        return lax.dynamic_slice_in_dim(x, me * count, count, axis)

    wq = pad_to(mine(w_qkv, 2, size), 2, sp)
    wq = jnp.transpose(wq, (1, 0, 2)).reshape(width, 3 * sp)
    wo = pad_to(mine(w_out, 0, size), 0, sp)
    wu = pad_to(mine(w_up, 1, ff), 1, ffp)
    wd = pad_to(mine(w_down, 0, ff), 0, ffp)
    bq = pad_to(mine(attn_bias, 1, size), 1, sp)
    bu = pad_to(mine(up_bias, 0, ff), 0, ffp)[None]
    consts = jnp.stack(
        [
            jnp.concatenate([bq[0], jnp.zeros_like(bq[0]), bq[1]]),
            jnp.concatenate([jnp.full((sp,), factor, F32), jnp.ones((2 * sp,), F32)]),
        ]
    )

    h1, qkv = first(shards, states, jnp.stack([norm_gain[0], norm_bias[0]]), wq, consts)
    grad_y = (cotangent.astype(F32) * valid).astype(BF16)
    gy = lax.all_gather(grad_y, "seq", axis=0)

    qkv = by_group(qkv)
    query, key, value = qkv[..., :sp], qkv[..., sp : 2 * sp], qkv[..., 2 * sp :]
    scores = jnp.where(same, mm("gqd,gkd->gqk", query, key), NEG)
    highest = jnp.max(scores, axis=-1, keepdims=True)
    weights = jnp.exp(scores - highest)
    totals = jnp.sum(weights, axis=-1, keepdims=True)
    attended = mm("gqk,gkd->gqd", weights.astype(BF16), value) / totals
    lse = highest + jnp.log(totals)
    att_b = attended.astype(BF16)
    att_mine = lax.all_to_all(att_b[..., :size], "seq", split_axis=1, concat_axis=2, tiled=True)

    mid, grad_mid, grad_att, grad_out, grad_up, grad_down, down_part, sums, up_sums = middle(
        shards, att_mine, states, gy, by_block(att_b),
        jnp.stack([norm_gain[1], norm_bias[1], attn_bias[2]]), bu, w_out, wo, wu, wd,
    )
    down = lax.psum_scatter(down_part, "seq", scatter_dimension=0, tiled=False).astype(F32)
    layer_out = ((mid + down + down_bias) * valid).astype(BF16)
    grad_att = by_group(grad_att)
    grad_out, grad_up, grad_down = grad_out[:size], grad_up[:ff], grad_down[:ff]

    delta = jnp.sum(grad_att.astype(F32) * attended, axis=-1, keepdims=True)
    scores2 = jnp.where(same, mm("gqd,gkd->gqk", query, key), NEG)
    probs = jnp.exp(scores2 - lse)
    grad_scores = (probs * (mm("gqd,gkd->gqk", grad_att, value) - delta)).astype(BF16)
    pre = jnp.stack(
        [
            (mm("gqk,gkd->gqd", grad_scores, key) * factor).astype(BF16),
            mm("gqk,gqd->gkd", grad_scores, query).astype(BF16),
            mm("gqk,gqd->gkd", probs.astype(BF16), grad_att).astype(BF16),
        ]
    )[..., :size]
    bias_sums = jnp.sum(pre.astype(F32), axis=(1, 2))
    grad_qkv = mm("gtd,cgte->cde", by_group(h1), pre)
    pre_mine = lax.all_to_all(pre, "seq", split_axis=2, concat_axis=3, tiled=True)
    grad_h1 = mm("cgte,cde->gtd", pre_mine, w_qkv)
    normed_one, scale_one = normalize(states.astype(F32))
    gain_one = jnp.sum(grad_h1 * normed_one, axis=(0, 1))
    shift_one = jnp.sum(grad_h1, axis=(0, 1))
    state_grad = (grad_mid + norm_back(grad_h1, normed_one, scale_one, norm_gain[0])).astype(BF16)

    qkv_rows = lax.all_to_all(grad_qkv.astype(BF16), "seq", split_axis=1, concat_axis=2, tiled=True)
    up_rows = lax.all_to_all(grad_up.T.astype(BF16), "seq", split_axis=0, concat_axis=1, tiled=True)
    wide = jnp.concatenate(
        [qkv_rows.reshape(-1, width), grad_out.astype(BF16), grad_down.astype(BF16)], axis=0
    )
    wide = lax.psum_scatter(wide, "dp", scatter_dimension=1, tiled=True).astype(F32)
    up_part = lax.psum_scatter(up_rows, "dp", scatter_dimension=1, tiled=True).astype(F32)
    vectors = lax.psum(jnp.stack([gain_one, sums[0], shift_one, sums[1], sums[2]]), ("dp", "seq"))
    vectors = mine(vectors, 1, size)
    pairs = lax.psum(
        (jnp.stack([bias_sums[0], bias_sums[2], mine(sums[3], 0, size)]), up_sums[0, :ff]), "dp"
    )
    narrow = wide.shape[1]
    return (
        layer_out,
        state_grad,
        wide[: 3 * size].reshape(3, size, narrow),
        wide[3 * size : 4 * size],
        jnp.stack([pairs[0][0], pairs[0][1], vectors[4]]),
        vectors[0:2],
        vectors[2:4],
        up_part,
        pairs[1],
        wide[4 * size :],
        pairs[0][2],
    )


def solution(mesh):
    placed = (P("dp", "seq", None), P("dp", None), P("dp", "seq", None)) + (P(),) * 9
    return jax.shard_map(
        body,
        mesh=mesh,
        in_specs=placed,
        out_specs=(
            P("dp", "seq", None), P("dp", "seq", None), P(None, "seq", "dp"), P("seq", "dp"),
            P(None, "seq"), P(None, "seq"), P(None, "seq"), P("seq", "dp"), P("seq"),
            P("seq", "dp"), P("seq"),
        ),
        check_vma=False,
    )
```

time: 609 us -> 383 us (0.63)
  waiting for transfers between devices: 375 us -> 61.8 us
  Pallas kernels: 0 us -> 131 us
  matrix products: 72.6 us -> 25.1 us
  other arithmetic: 27.1 us -> 13.9 us
  local copies, waits for them, and re-layouts: 48.4 us -> 57.1 us
  blocking collectives: 45.5 us -> 51.8 us
    all_gather x4 -> x1, waiting for transfers between devices: 201 us -> 0.01 us  [body(): gy = lax.all_gather(grad_y, 'seq', axis=0)]
    pallas_call x0 -> x2, Pallas kernels: none -> 131 us  [the longest x1 92 us: middle(): pl.pallas_call(functools.partial(middle_kernel, shards), out_shape=[sds((...]
    reduce_scatter x2 -> x1, waiting for transfers between devices: 143 us -> 18.5 us  [body(): lax.psum_scatter(down_part, 'seq', scatter_dimension=0, tiled=False)]
    dot_general x18 -> x8, matrix products: 72.6 us -> 25.1 us  [mm(): return jnp.einsum(spec, a, b, preferred_element_type=F32)]
    all_to_all x1, waiting for transfers between devices: 0.01 us -> 24.2 us  [body(): lax.all_to_all(pre, 'seq', split_axis=2, concat_axis=3, tiled=True)]
    unnamed x10 -> x6, waiting for transfers between devices: 15.4 us -> 0.54 us
    reduce_sum x3 -> x1, other arithmetic: 7.81 us -> 1.37 us  [body(): delta = jnp.sum(grad_att.astype(F32) * attended, axis=-1, keepdims=True)]
    psum x2, blocking collectives: 45.5 us -> 51.8 us  [the longest x1 46.2 us: body(): lax.psum(jnp.stack([gain_one, sums[0], shift_one, sums[1], sums[2]]), ('d...]
  transfers between devices with their start and end apart: 12 -> 8, of which waited for: 9 -> 4; matrix products, arithmetic and copies ran while one was open for 15% -> 19% of each run, Pallas kernels for 0% -> 10%
where the time goes in v2:
time: 383 us; the launch traced here: 376 us
  Pallas kernels  131 us (34%)
  waiting for transfers between devices  61.8 us (16%)
  local copies, waits for them, and re-layouts  57.1 us (15%)
  blocking collectives  51.8 us (14%)
  matrix products  25.1 us (7%)
  starting transfers between devices  19.8 us (5%)
  between operations  15.4 us (4%)
  other arithmetic  13.9 us (4%)
    pallas_call x1, Pallas kernels, middle(): pl.pallas_call(functools.partial(middle_kernel, shards), out_shape=[sds((...  92 us
    psum x1, blocking collectives, body(): lax.psum(jnp.stack([gain_one, sums[0], shift_one, sums[1], sums[2]]), ('d...  46.2 us
    pallas_call x1, Pallas kernels, first(): pl.pallas_call(functools.partial(first_kernel, shards), out_shape=[jax.Sh...  39.1 us
    dot_general x8, matrix products, mm(): return jnp.einsum(spec, a, b, preferred_element_type=F32)  25.1 us
    all_to_all x1, waiting for transfers between devices, body(): lax.all_to_all(pre, 'seq', split_axis=2, concat_axis=3, tiled=True)  24.2 us
    reduce_scatter x1, waiting for transfers between devices, body(): lax.psum_scatter(down_part, 'seq', scatter_dimension=0, tiled=False)  18.5 us
    unnamed x43, local copies, waits for them, and re-layouts  11.5 us
    all_to_all x1, waiting for transfers between devices, body(): lax.all_to_all(grad_up.T.astype(BF16), 'seq', split_axis=0, concat_axis=1...  10.3 us
  transfers between devices with their start and end apart: 8, of which 4 were waited for; matrix products, arithmetic and copies ran while one was open for 19% of the time, Pallas kernels for 10%

profile of v2, /device:TPU:0, one launch (start us, length us, event | category | flops | bytes accessed | tf_op | source)
XLA Modules:
  0.0 376.1 jit_solution(1064083385227354217)
XLA Ops:
  8.3 1.8 multiply_convert_fusion.1
  11.0 1.8 constant_dynamic-slice_fusion.7
  14.2 39.1 %first.1 = (bf16[16,2,64,1152]{3,2,1,0:T(8,128)(2,1)S(1)}, bf16[16,2,64,384]{3,2,1,0:T(8,128)(2,1)S(1)}) custom-call(bf16[2,64,1152]{2,1,0:T(8,128)(2,1)S(1)} %copy-done, f32[2,1152]{1,0:T(2,128)S(1)} %pad_maximum_fusion.5.vec_ref, bf16[1152,384]{1,0:T(8,128)(2,1)S(1)} %copy.115.w_ref, f32[2,384]{1,0:T(2,128)S(1)} %pad_maximum_fusion.6.b_ref), custom_call_target="tpu_custom_call" | custom-call | tf_op jit(solution)/shard_map/first/pallas_call | solution.py:249
  53.5 1.5 fusion.5
  55.5 1.8 fusion.2
  57.3 3.1 fusion.58
  60.4 1.1 copy.119
  61.5 5.5 %all-to-all-start = ((bf16[2,1024,72]{2,0,1:T(2,128)(2,1)}), bf16[2,1024,72]{2,0,1:T(2,128)(2,1)}, u32[]{:S(2)}, u32[]{:S(2)}) async-start(bf16[2,1024,72]{2,0,1:T(2,128)(2,1)} %copy.119), calls=%async_computation | async-start | bytes 1048576 | tf_op jit(solution)/shard_map/all_to_all | solution.py:449
  67.0 2.1 constant_dynamic-slice_fusion.3
  69.0 1.2 constant_dynamic-slice_fusion.2
  75.0 1.5 copy.164
  78.5 5.0 %copy.138 = bf16[2,16,64,1152]{3,2,1,0:T(8,128)(2,1)} copy(bf16[2,16,64,1152]{3,2,0,1:T(8,128)(2,1)} %bitcast.91) | data formatting | bytes 9437184 | tf_op jit(solution)/shard_map/transpose | solution.py:417
  85.0 1.4 copy.171
  86.4 1.2 all_to_all.54.att_ref
  87.6 92.0 %middle.1 = (f32[2,64,1152]{2,1,0:T(8,128)}, f32[2,64,1152]{2,1,0:T(8,128)}, bf16[16,2,64,128]{3,2,1,0:T(8,128)(2,1)}, f32[128,1152]{1,0:T(8,128)}, f32[384,1152...) custom-call(bf16[2,64,1152]{2,1,0:T(8,128)(2,1)} %all_to_all.54.att_, ...), custom_call_target="tpu_custom_call" | custom-call | tf_op jit(solution)/shard_map/middle/pallas_call | solution.py:370
  179.6 1.1 copy.125
  181.1 1.4 multiply_reduce_fusion
  182.5 4.7 %multiply_convert_fusion = bf16[2,1024,1024]{1,2,0:T(8,128)(2,1)S(1)} fusion(f32[2,1024,1024]{1,2,0:T(8,128)} %copy-done.3, f32[2,1024]{1,0:T(2,128)S(1)} %multiply_reduce_fusion, f32[2,1024]{1,0:T(2,128)S(1)} %log_add_fusion, s32[2,1024]{1,0:T(2,128)S(1)} %convert_reduce_fusion.2, bf16[2,1024,128]{2,1,0:T(8,128)(2,1)S(1)} %bitcast.115, ...), kind=kOutput, calls=%fused_computation | convolution fusion | flops 549453824 | bytes 13664256 | tf_op jit(solution)/shard_map/gqd,gkd->gqk/dot_general | solution.py:22
  187.1 1.5 fusion.23
  188.7 1.6 fusion.19
  190.3 1.4 fusion.32
  191.6 1.3 copy.141
  192.9 4.1 %all-to-all-start.3 = ((bf16[16,72,269]{2,1,0:T(8,128)(2,1)}), bf16[16,72,269]{2,1,0:T(8,128)(2,1)S(1)}, u32[]{:S(2)}, u32[]{:S(2)}) async-start(bf16[16,72,269]{2,1,0:T(8,128)(2,1)} %bitcast.34), calls=%async_computation.4 | async-start | bytes 1769472 | tf_op jit(solution)/shard_map/all_to_all | solution.py:481
  197.0 5.5 %fusion.20 = bf16[1,2,1024,128]{2,3,1,0:T(8,128)(2,1)S(1)} fusion(bf16[2,1024,128]{2,1,0:T(8,128)(2,1)S(1)} %bitcast.116, f32[2,1024,1024]{1,2,0:T(8,128)} %copy-done.3, f32[2,1024]{1,0:T(2,128)S(1)} %log_add_fusion, s32[2,1024]{1,0:T(2,128)S(1)} %convert_reduce_fusion.2), kind=kOutput, calls=%fused_computation.26 | convolution fusion | flops 545521664 | bytes 9453568 | tf_op jit(solution)/shard_map/gqk,gqd->gkd/dot_general | solution.py:22
  202.7 1.3 fusion.14
  204.9 2.0 reshape.111
  206.9 10.3 %all-to-all-done.3 = bf16[16,72,269]{2,1,0:T(8,128)(2,1)S(1)} async-done(((bf16[16,72,269]{2,1,0:T(8,128)(2,1)}), bf16[16,72,269]{2,1,0:T(8,128)(2,1)S(1)}, u32[]{:S(2)}, u32[]{:S(2)}) %all-to-all-start.3) | async-done | bytes 619808 | tf_op jit(solution)/shard_map/all_to_all | solution.py:481
  217.2 6.0 %all-to-all-start.2 = ((bf16[16,2,7776]{2,1,0:T(2,128)(2,1)}), bf16[16,2,7776]{2,1,0:T(2,128)(2,1)S(1)}, u32[]{:S(2)}, u32[]{:S(2)}) async-start(bf16[16,2,7776]{2,1,0:T(2,128)(2,1)} %reshape.111), calls=%async_computation.3 | async-start | bytes 999424 | tf_op jit(solution)/shard_map/all_to_all | solution.py:480
  223.4 1.6 all_to_all.65
  225.1 1.7 slice.161
  226.8 2.2 slice.160
  229.0 8.2 %all-to-all-done.2 = bf16[16,2,7776]{2,1,0:T(2,128)(2,1)S(1)} async-done(((bf16[16,2,7776]{2,1,0:T(2,128)(2,1)}), bf16[16,2,7776]{2,1,0:T(2,128)(2,1)S(1)}, u32[]{:S(2)}, u32[]{:S(2)}) %all-to-all-start.2) | async-done | bytes 497696 | tf_op jit(solution)/shard_map/all_to_all | solution.py:480
  237.2 1.9 reshape.112
  240.5 1.2 pad_maximum_fusion
  241.7 1.6 copy.158
  244.1 2.9 copy.135
  247.0 4.1 %all-to-all-start.1 = ((bf16[3,2,1024,72]{3,1,0,2:T(2,128)(2,1)}), bf16[3,2,1024,72]{3,1,0,2:T(2,128)(2,1)S(1)}, u32[]{:S(2)}, u32[]{:S(2)}) async-start(bf16[3,2,1024,72]{3,1,0,2:T(2,128)(2,1)} %copy.135), calls=%async_computation.2 | async-start | bytes 3145728 | tf_op jit(solution)/shard_map/all_to_all | solution.py:473
  252.8 5.6 %all-reduce.7 = (f32[3,72]{1,0:T(4,128)S(1)}, f32[269]{0:T(512)}) all-reduce(f32[3,72]{1,0:T(4,128)S(1)} %pad_maximum_fusion.8, f32[269]{0:T(512)S(1)} %slice_reduce_fusion), channel_id=1, replica_groups=mesh['dp'=2,'seq'=16] {'dp'}, use_global_device_ids=true, to_apply=%region_12.13 | all-reduce | flops 485 | bytes 3880 | tf_op jit(solution)/shard_map/psum | solution.py:489
  258.9 24.2 %all-to-all-done.1 = bf16[3,2,1024,72]{3,1,0,2:T(2,128)(2,1)S(1)} async-done(((bf16[3,2,1024,72]{3,1,0,2:T(2,128)(2,1)}), bf16[3,2,1024,72]{3,1,0,2:T(2,128)(2,1)S(1)}, u32[]{:S(2)}, u32[]{:S(2)}) %all-to-all-start.1) | async-done | bytes 884768 | tf_op jit(solution)/shard_map/all_to_all | solution.py:473
  284.2 1.7 all_to_all.58
  285.9 6.0 %fusion.38 = (f32[1152]{0:T(1024)S(1)}, f32[2,64]{1,0:T(2,128)S(1)}, f32[2,64]{1,0:T(2,128)S(1)}, f32[1152]{0:T(1024)S(1)}, f32[2,64,1152]{2,1,0:T(8,128)S(1)}) fusion(bf16[2,64,1152]{2,1,0:T(8,128)(2,1)S(1)} %copy-done.1, f32[2,64]{1,0:T(2,128)S(1)} %add_rsqrt_fusion, f32[2,64]{1,0:T(2,128)S(1)} %broadcast_multiply_fusion.2, ...), kind=kOutput, calls=%fused_computation.46 | convolution fusion | flops 1020687872 | bytes 9747968 | tf_op jit(solution)/shard_map/cgte,cde->gtd/dot_general | solution.py:22
  292.0 46.2 %psum.22 = f32[5,1152]{1,0:T(8,128)S(1)} all-reduce(f32[5,1152]{1,0:T(8,128)S(1)} %pad_maximum_fusion.3), channel_id=1, replica_groups=mesh['dp'=2,'seq'=16] {'dp','seq'}, use_global_device_ids=true, to_apply=%region_15.16 | all-reduce | flops 5760 | bytes 46080 | tf_op jit(solution)/shard_map/psum | solution.py:487
  340.5 2.0 dynamic-slice_convert_fusion
  342.5 1.1 slice.131
  344.6 1.2 slice.133
  347.6 1.2 copy.175
  348.8 18.5 %reduce-scatter.6.cloned.1.call-done = bf16[1,2,64,1152]{3,2,1,0:T(8,128)(2,1)} async-done(((bf16[16,2,64,1152]{3,2,1,0:T(8,128)(2,1)}), bf16[1,2,64,1152]{3,2,1,0:T(8,128)(2,1)}) %reduce-scatter.6.cloned.1.call-update) | async-done | bytes 294928 | tf_op jit(solution)/shard_map/reduce_scatter | solution.py:455
  367.3 1.8 fusion.42
  (108 shorter events, 23.6 us)
Async XLA Ops:
  7.2 6.9 %copy-start.13 = (f32[1,384]{1,0:T(1,128)S(1)}, f32[1,384]{1,0:T(1,128)}, u32[]{:S(2)}) copy-start(f32[1,384]{1,0:T(1,128)} %constant.14.clone.1) | copy-start | bytes 4612
  7.2 6.9 %copy-start.9 = (f32[2,1152]{1,0:T(2,128)S(1)}, f32[2,1152]{1,0:T(2,128)}, u32[]{:S(2)}) copy-start(f32[2,1152]{1,0:T(2,128)} %param.18) | copy-start | bytes 27652
  7.2 7.0 %copy-start.10 = (f32[2,1152]{1,0:T(2,128)S(1)}, f32[2,1152]{1,0:T(2,128)}, u32[]{:S(2)}) copy-start(f32[2,1152]{1,0:T(2,128)} %param.19) | copy-start | bytes 27652
  7.2 7.0 %copy-start = (bf16[2,64,1152]{2,1,0:T(8,128)(2,1)S(1)}, bf16[2,64,1152]{2,1,0:T(8,128)(2,1)}, u32[]{:S(2)}) copy-start(bf16[2,64,1152]{2,1,0:T(8,128)(2,1)} %x_ref.3) | copy-start | bytes 884740
  7.2 80.4 %all-gather.3.cloned.1.call-start = ((), (), s32[]{:S(2)}) async-start(), calls=%async_computation.7 | async-start | bytes 5013504 | tf_op jit(solution)/shard_map/all_gather | solution.py:438
  53.3 2.1 copy-start.2
  55.5 4.9 %copy-start.3 = (f32[2,1024,1024]{1,2,0:T(8,128)}, f32[2,1024,1024]{1,2,0:T(8,128)S(1)}, u32[]{:S(2)}) copy-start(f32[2,1024,1024]{1,2,0:T(8,128)S(1)} %get-tuple-element.55) | copy-start | bytes 25165828
  61.5 23.5 %all-to-all-start = ((bf16[2,1024,72]{2,0,1:T(2,128)(2,1)}), bf16[2,1024,72]{2,0,1:T(2,128)(2,1)}, u32[]{:S(2)}, u32[]{:S(2)}) async-start(bf16[2,1024,72]{2,0,1:T(2,128)(2,1)} %copy.119), calls=%async_computation | async-start | bytes 1048576 | tf_op jit(solution)/shard_map/all_to_all | solution.py:449
  78.5 5.0 %copy-start.4 = (bf16[2,1024,128]{2,1,0:T(8,128)(2,1)S(1)}, bf16[2,1024,128]{2,1,0:T(8,128)(2,1)}, u32[]{:S(2)}) copy-start(bf16[2,1024,128]{2,1,0:T(8,128)(2,1)} %copy.122) | copy-start | bytes 1572868
  192.9 9.8 %slice-start = ((s8[4718592]{0:T(1024)(128)(4,1)}), s8[524288]{0:T(1024)(128)(4,1)S(1)}, s32[]{:S(2)}) async-start(s8[4718592]{0:T(1024)(128)(4,1)} %bitcast.103), calls=%async_computation.10 | async-start | bytes 1048576
  192.9 24.4 %all-to-all-start.3 = ((bf16[16,72,269]{2,1,0:T(8,128)(2,1)}), bf16[16,72,269]{2,1,0:T(8,128)(2,1)S(1)}, u32[]{:S(2)}, u32[]{:S(2)}) async-start(bf16[16,72,269]{2,1,0:T(8,128)(2,1)} %bitcast.34), calls=%async_computation.4 | async-start | bytes 1769472 | tf_op jit(solution)/shard_map/all_to_all | solution.py:481
  197.0 5.5 %copy-start.7 = (bf16[1,2,1024,128]{2,3,1,0:T(8,128)(2,1)S(1)}, bf16[1,2,1024,128]{2,3,1,0:T(8,128)(2,1)}, u32[]{:S(2)}) copy-start(bf16[1,2,1024,128]{2,3,1,0:T(8,128)(2,1)} %fusion.19) | copy-start | bytes 1572868
  197.0 5.7 %slice-start.1 = ((s8[4718592]{0:T(1024)(128)(4,1)}), s8[4194304]{0:T(1024)(128)(4,1)S(1)}, s32[]{:S(2)}) async-start(s8[4718592]{0:T(1024)(128)(4,1)} %bitcast.103), calls=%async_computation.11 | async-start | bytes 8388608
  217.2 19.9 %all-to-all-start.2 = ((bf16[16,2,7776]{2,1,0:T(2,128)(2,1)}), bf16[16,2,7776]{2,1,0:T(2,128)(2,1)S(1)}, u32[]{:S(2)}, u32[]{:S(2)}) async-start(bf16[16,2,7776]{2,1,0:T(2,128)(2,1)} %reshape.111), calls=%async_computation.3 | async-start | bytes 999424 | tf_op jit(solution)/shard_map/all_to_all | solution.py:480
  223.3 117.3 %all-reduce.10.cloned.1.call-start = ((), (), s32[]{:S(2)}) async-start(), calls=%async_computation.9 | async-start | bytes 1253376
  225.1 117.4 %reduce-scatter.8.cloned.1.call-start = ((), (), s32[]{:S(2)}) async-start(), calls=%async_computation.8 | async-start | bytes 2211840
  241.7 2.3 copy-start.1
  243.4 123.9 %reduce-scatter.6.cloned.1.call-start = ((), (), s32[]{:S(2)}) async-start(), calls=%async_computation.6 | async-start | bytes 5013504 | tf_op jit(solution)/shard_map/reduce_scatter | solution.py:455
  243.5 7.7 %copy-start.14 = (u32[32]{0:T(128)S(1)}, u32[32]{0:T(128)}, u32[]{:S(2)}) copy-start(u32[32]{0:T(128)} %constant.60) | copy-start | bytes 388
  243.5 9.2 %copy-start.8 = (f32[8,1152]{1,0:T(8,128)S(1)}, f32[8,1152]{1,0:T(8,128)}, u32[]{:S(2)}) copy-start(f32[8,1152]{1,0:T(8,128)} %get-tuple-element.30) | copy-start | bytes 110596
  243.5 9.3 %copy-start.12 = (f32[1,384]{1,0:T(1,128)S(1)}, f32[1,384]{1,0:T(1,128)}, u32[]{:S(2)}) copy-start(f32[1,384]{1,0:T(1,128)} %get-tuple-element.32) | copy-start | bytes 4612
  247.0 36.1 %all-to-all-start.1 = ((bf16[3,2,1024,72]{3,1,0,2:T(2,128)(2,1)}), bf16[3,2,1024,72]{3,1,0,2:T(2,128)(2,1)S(1)}, u32[]{:S(2)}, u32[]{:S(2)}) async-start(bf16[3,2,1024,72]{3,1,0,2:T(2,128)(2,1)} %copy.135), calls=%async_computation.2 | async-start | bytes 3145728 | tf_op jit(solution)/shard_map/all_to_all | solution.py:473
  285.9 53.6 %copy-start.5 = (f32[2,64,1152]{2,1,0:T(8,128)S(1)}, f32[2,64,1152]{2,1,0:T(8,128)}, u32[]{:S(2)}) copy-start(f32[2,64,1152]{2,1,0:T(8,128)} %get-tuple-element.25) | copy-start | bytes 1769476
  339.5 27.8 %copy-start.6 = (f32[2,64,1152]{2,1,0:T(8,128)S(1)}, f32[2,64,1152]{2,1,0:T(8,128)}, u32[]{:S(2)}) copy-start(f32[2,64,1152]{2,1,0:T(8,128)} %get-tuple-element.23) | copy-start | bytes 1769476
  339.5 27.8 %copy-start.11 = (f32[1152]{0:T(1024)S(1)}, f32[1152]{0:T(1024)}, u32[]{:S(2)}) copy-start(f32[1152]{0:T(1024)} %param.23) | copy-start | bytes 13828
Sparse Core Ops, SparseCore 0:
  10.9 69.5 all-gather.2
  227.0 32.6 all-reduce.9
  261.9 25.2 reduce-scatter.7
  290.9 76.3 reduce-scatter.5
